TPU v7x, 512 devices: a whole 4x8x8 slice. The times are simulated.
512 devices in a mesh: member: 8 (over y_hi, core), space: 64 (over x, y_lo, z).
Axes of the slice: x: 4, y: 8 (y_hi: 4, y_lo: 2; y = y_hi * 2 + y_lo), z: 8, core: 2. Of those that a mesh axis runs over, the one named last changes fastest.
Arguments:
- mean_logk: float32 [256, 128, 256], P('space'), may hold values from -2.5 to 2.5
- perturbation: float32 [8, 256, 128, 256], P('member', 'space'), may hold values from -2.5 to 2.5
- start_conc: float32 [8, 256, 128, 256], P('member', 'space'), may hold values from 0 to 1
- source_mask: int32 [8, 256, 128, 256], P('member', 'space'), may hold values 0 or 1
- control_x: int32 [128, 256], replicated, may hold values from 0 to 255
- observed: float32 [8, 8], P('member'), may hold values from -4 to 4
Outputs:
- updated_logk: float32 [256, 128, 256], P('space')
- misfit: float32 [], replicated
All inputs are finite; a program needn't handle non-finite values. No bound on the sum of `source_mask` on one device may be relied on, other than what follows from the above.
Results may differ from a plain program's by a relative error of at most 0.0003.
Values sent between devices are 32-bit elements; how exact they have to be, the bound alone decides.
A program may use at most 64 MiB of HBM per device.

v0:
```python
import jax
import jax.numpy as jnp
from jax import lax
from jax.sharding import PartitionSpec as P

NOBS = 8


time_step = 0.015
dissolve_rate = 15.0
descent_rate = 0.5
epsilon = 1e-06


def extended_2(shard, sides, width):
    for axis, dim in sides:
        devices, length = (lax.axis_size(axis), shard.shape[dim])
        up = [(i, (i + 1) % devices) for i in range(devices - 1)]
        down = [(j, i) for i, j in up]
        last = lax.slice_in_dim(shard, length - width, length, axis=dim)
        leading = lax.slice_in_dim(shard, 0, width, axis=dim)
        before = lax.ppermute(last, axis, up)
        after = lax.ppermute(leading, axis, down)
        shard = jnp.concatenate([before, shard, after], axis=dim)
    return shard


def shift_cells(values, axis, offset):
    length = values.shape[axis]
    zero = jnp.zeros_like(lax.slice_in_dim(values, 0, 1, axis=axis))
    if offset > 0:
        return jnp.concatenate([lax.slice_in_dim(values, 1, length, axis=axis), zero], axis)
    return jnp.concatenate([zero, lax.slice_in_dim(values, 0, length - 1, axis=axis)], axis)


def neighbours(extended):
    centre = extended[1:-1]
    beside_all = [extended[2:], extended[:-2]]
    for axis in (1, 2):
        for offset in (1, -1):
            beside_all.append(shift_cells(centre, axis, offset))
    return (centre, beside_all)


def flow(field_ext, coef_ext):
    field, field_nb = neighbours(field_ext)
    coef, coef_nb = neighbours(coef_ext)
    total = jnp.zeros_like(field)
    for value_n, coef_n in zip(field_nb, coef_nb):
        total = total + 0.5 * (coef + coef_n) * (value_n - field)
    return total


def transport(conc_ext, coef_ext, maskf):
    conc = conc_ext[1:-1]
    return (
        conc
        + time_step * flow(conc_ext, coef_ext)
        + time_step * dissolve_rate * maskf * (1.0 - conc)
    )


def adjoint_step(adjoint_ext, coef_ext, maskf):
    adjoint = adjoint_ext[1:-1]
    return (
        adjoint
        + time_step * flow(adjoint_ext, coef_ext)
        - time_step * dissolve_rate * maskf * adjoint
    )


def sensitivity(adjoint_ext, state_ext):
    adjoint, adjoint_nb = neighbours(adjoint_ext)
    state, state_nb = neighbours(state_ext)
    total = jnp.zeros_like(adjoint)
    for lam_n, state_n in zip(adjoint_nb, state_nb):
        total = total + (lam_n - adjoint) * (state_n - state)
    return -0.5 * time_step * total


def select_rows(start_x, count, control_x):
    rows_x = start_x + jnp.arange(count, dtype=jnp.int32)
    return (rows_x[:, None, None] == control_x[None]).astype(jnp.float32)


def shards(mean_logk, perturbation, start_conc, source_mask, control_x, observed):
    slab = mean_logk.shape[0]
    ny_cells = mean_logk.shape[1]
    nz_cells = mean_logk.shape[2]
    slabs = lax.axis_size("space")
    members = lax.axis_size("member")
    first = lax.axis_index("space") * slab
    conduct = jnp.exp(mean_logk + perturbation[0])
    maskf = source_mask[0].astype(jnp.float32)
    conc = start_conc[0]
    joined = extended_2(jnp.stack([conduct, conc]), (("space", 1),), 1)
    coef_ext = joined[0]
    start_ext = joined[1]
    first_state = transport(start_ext, coef_ext, maskf)
    first_ext = extended_2(first_state, (("space", 0),), 1)
    second = transport(first_ext, coef_ext, maskf)
    select = select_rows(first, slab, control_x)
    column = jnp.sum(select * conduct * second, axis=0)
    columns = ny_cells * nz_cells // NOBS
    partial_value = column.reshape(NOBS, -1).sum(axis=1) / columns
    totals = lax.psum(partial_value, "space")
    resid = totals - observed[0]
    weight = jnp.repeat(resid, ny_cells // NOBS)[None, :, None]
    grad_k = select * weight * second
    adjoint = select * weight * conduct
    for state_ext, further in ((first_ext, True), (start_ext, False)):
        adjoint_ext = extended_2(adjoint, (("space", 0),), 1)
        grad_k = grad_k + sensitivity(adjoint_ext, state_ext)
        if further:
            adjoint = adjoint_step(adjoint_ext, coef_ext, maskf)
    grad_m = conduct * grad_k
    misfit_part = 0.5 * jnp.sum(resid * resid) / (members * NOBS)
    cells = slab * slabs * ny_cells * nz_cells
    total, misfit = lax.psum((grad_m, misfit_part), "member")
    squares = lax.psum(jnp.sum(total * total), "space")
    updated = mean_logk - descent_rate * total * lax.rsqrt(squares / cells + epsilon)
    return (updated, misfit)


def solution(mesh):
    in_specs = (
        P("space", None, None),
        P("member", "space", None, None),
        P("member", "space", None, None),
        P("member", "space", None, None),
        P(),
        P("member", None),
    )
    out_specs = (P("space", None, None), P())
    return jax.shard_map(shards, mesh=mesh, in_specs=in_specs, out_specs=out_specs, check_vma=False)
```

profile of v0, /device:TPU:32, one launch (start us, length us, event | category | flops | bytes accessed | tf_op | source)
XLA Modules:
  0.0 479.4 jit_solution(13472112534503990203)
XLA Ops:
  7.2 0.0 copy-start
  7.2 0.0 all-reduce.22.cloned.1.call-start
  7.2 1.3 fusion.30
  8.6 0.0 copy-done
  8.6 0.8 pad_maximum_fusion.10
  9.3 4.3 collective-permute-start.1
  13.6 1.3 collective-permute-start
  14.9 0.1 fusion.41
  15.1 0.0 copy-start.5
  15.1 0.0 copy-start.7
  15.1 0.0 copy-start.3
  15.1 0.3 fusion.40
  15.5 0.0 copy-start.9
  15.5 0.0 copy-start.11
  15.5 0.0 copy-start.1
  15.5 4.0 collective-permute-done.1
  19.5 4.4 collective-permute-done
  23.9 0.7 copy-done.21
  24.6 0.0 copy-done.5
  24.6 0.0 copy-done.7
  24.6 0.0 copy-done.3
  24.6 1.8 fusion.27
  26.4 0.0 copy-done.9
  26.5 0.2 fusion.38
  26.7 4.3 collective-permute-start.3
  31.0 0.0 copy-start.26
  31.0 1.4 collective-permute-start.2
  32.4 0.1 fusion.39
  32.5 0.9 collective-permute-done.3
  33.5 6.1 %collective-permute-done.2 = f32[1,128,256]{2,1,0:T(8,128)S(1)} collective-permute-done((f32[1,128,256]{2,1,0:T(8,128)S(1)}, f32[1,128,256]{2,1,0:T(8,128)S(1)}, u32[]{:S(2)}, u32[]{:S(2)}) %collective-permute-start.2) | collective-permute-done | bytes 131104 | tf_op jit(solution)/shard_map/ppermute | solution.py:23
  39.6 0.6 copy-done.29
  40.2 1.0 fusion.1
  41.2 0.1 reduce_sum.39
  41.3 0.1 reduce_sum.40
  41.4 0.0 copy-start.31
  41.4 156.3 %psum.28 = f32[8]{0:T(128)S(1)} all-reduce(f32[8]{0:T(128)S(1)} %broadcast_multiply_fusion), channel_id=1, replica_groups=mesh['member'=8,'space'=64] {'space'}, use_global_device_ids=true, to_apply=%region_2.0 | all-reduce | flops 8 | bytes 64 | tf_op jit(solution)/shard_map/psum | solution.py:106
  197.8 0.6 multiply_reduce_fusion.1
  198.4 0.1 broadcast_in_dim.2
  198.5 0.1 mul.227
  198.5 0.1 select_multiply_fusion
  198.7 0.2 fusion.35
  198.9 1.3 collective-permute-start.5
  200.2 0.0 copy-start.2
  200.2 0.0 copy-start.4
  200.2 1.4 collective-permute-start.4
  201.7 0.1 fusion.36
  201.8 0.9 collective-permute-done.5
  202.7 4.5 collective-permute-done.4
  207.2 0.0 copy-done.4
  207.3 0.9 fusion.29
  208.2 0.1 fusion.31
  208.3 1.4 collective-permute-start.6
  209.8 4.7 collective-permute-start.7
  214.5 0.2 fusion.32
  214.7 0.6 collective-permute-done.6
  215.3 1.7 collective-permute-done.7
  217.0 0.0 copy-done.16
  217.0 3.3 fusion.4
  220.4 0.0 all-reduce.22.cloned.1.call-update
  221.1 71.3 %all-reduce.22.cloned.1.call-done = f32[4,128,256]{2,1,0:T(8,128)} async-done(((f32[4,128,256]{2,1,0:T(8,128)}), f32[4,128,256]{2,1,0:T(8,128)}) %all-reduce.22.cloned.1.call-update) | async-done | bytes 524304 | tf_op jit(solution)/shard_map/psum | solution.py:119
  292.4 1.9 multiply_reduce_fusion
  294.3 17.6 %psum.31 = f32[]{:T(128)} all-reduce(f32[]{:T(128)S(6)} %div.11), channel_id=1, replica_groups=mesh['member'=8,'space'=64] {'member'}, use_global_device_ids=true, to_apply=%region_7.0 | all-reduce | flops 1 | bytes 8 | tf_op jit(solution)/shard_map/psum | solution.py:119
  311.9 159.1 %psum.30 = f32[]{:T(128)} all-reduce(f32[]{:T(128)} %multiply_reduce_fusion), channel_id=1, replica_groups=mesh['member'=8,'space'=64] {'space'}, use_global_device_ids=true, to_apply=%region_5.0 | all-reduce | flops 1 | bytes 8 | tf_op jit(solution)/shard_map/psum | solution.py:120
  471.7 0.9 multiply_subtract_fusion
  (49 shorter events, 0.2 us)
Async XLA Ops:
  7.2 1.4 copy-start
  7.2 285.2 %all-reduce.22.cloned.1.call-start = ((), (), s32[]{:S(2)}) async-start(), calls=%async_computation | async-start | bytes 1048576 | tf_op jit(solution)/shard_map/psum | solution.py:119
  9.3 10.1 %collective-permute-start.1 = (f32[2,1,128,256]{3,2,1,0:T(8,128)}, f32[2,1,128,256]{3,2,1,0:T(8,128)S(1)}, u32[]{:S(2)}, u32[]{:S(2)}) collective-permute-start(f32[2,1,128,256]{3,2,1,0:T(8,128)} %get-tuple-element.4), channel_id=1, source_target_pairs={{0,1},{1,2},{2,3},{3,4},{4,5},{5,6},{6,7},{7,8},{8,9},{9,10},{10,1... | collective-permute-start | bytes 786440 | tf_op jit(solution)/shard_map/ppermute | solution.py:22
  13.6 10.3 %collective-permute-start = (f32[2,1,128,256]{3,2,1,0:T(8,128)S(1)}, f32[2,1,128,256]{3,2,1,0:T(8,128)S(1)}, u32[]{:S(2)}, u32[]{:S(2)}) collective-permute-start(f32[2,1,128,256]{3,2,1,0:T(8,128)S(1)} %get-tuple-element.5), channel_id=1, source_target_pairs={{1,0},{2,1},{3,2},{4,3},{5,4},{6,5},{7,6},{8,7},{9,8},{10,9},{11,1... | collective-permute-start | bytes 786440 | tf_op jit(solution)/shard_map/ppermute | solution.py:23
  15.1 9.5 %copy-start.5 = (f32[4,127,256]{2,1,0:T(8,128)}, f32[4,127,256]{2,1,0:T(8,128)S(1)}, u32[]{:S(2)}) copy-start(f32[4,127,256]{2,1,0:T(8,128)S(1)} %get-tuple-element.34) | copy-start | bytes 1560580
  15.1 9.5 %copy-start.7 = (f32[4,127,256]{2,1,0:T(8,128)}, f32[4,127,256]{2,1,0:T(8,128)S(1)}, u32[]{:S(2)}) copy-start(f32[4,127,256]{2,1,0:T(8,128)S(1)} %get-tuple-element.35) | copy-start | bytes 1560580
  15.1 9.5 %copy-start.3 = (s32[1,4,128,256]{3,2,1,0:T(8,128)S(1)}, s32[1,4,128,256]{3,2,1,0:T(8,128)}, u32[]{:S(2)}) copy-start(s32[1,4,128,256]{3,2,1,0:T(8,128)} %param.9) | copy-start | bytes 1572868
  15.5 11.0 %copy-start.9 = (f32[4,128,255]{2,1,0:T(8,128)}, f32[4,128,255]{2,1,0:T(8,128)S(1)}, u32[]{:S(2)}) copy-start(f32[4,128,255]{2,1,0:T(8,128)S(1)} %get-tuple-element.32) | copy-start | bytes 1566724
  15.5 11.0 %copy-start.11 = (f32[4,128,255]{2,1,0:T(8,128)}, f32[4,128,255]{2,1,0:T(8,128)S(1)}, u32[]{:S(2)}) copy-start(f32[4,128,255]{2,1,0:T(8,128)S(1)} %get-tuple-element.33) | copy-start | bytes 1566724
  15.5 24.1 %copy-start.1 = (f32[4,128,255]{2,1,0:T(8,128)}, f32[4,128,255]{2,1,0:T(8,128)S(1)}, u32[]{:S(2)}) copy-start(f32[4,128,255]{2,1,0:T(8,128)S(1)} %get-tuple-element.25) | copy-start | bytes 1566724
  23.9 0.7 copy-start.21
  26.7 12.9 %copy-start.13 = (f32[4,128,255]{2,1,0:T(8,128)}, f32[4,128,255]{2,1,0:T(8,128)S(1)}, u32[]{:S(2)}) copy-start(f32[4,128,255]{2,1,0:T(8,128)S(1)} %get-tuple-element.20) | copy-start | bytes 1566724
  26.7 12.9 %copy-start.15 = (f32[4,128,255]{2,1,0:T(8,128)}, f32[4,128,255]{2,1,0:T(8,128)S(1)}, u32[]{:S(2)}) copy-start(f32[4,128,255]{2,1,0:T(8,128)S(1)} %get-tuple-element.21) | copy-start | bytes 1566724
  26.7 6.8 %collective-permute-start.3 = (f32[1,128,256]{2,1,0:T(8,128)S(1)}, f32[1,128,256]{2,1,0:T(8,128)S(1)}, u32[]{:S(2)}, u32[]{:S(2)}) collective-permute-start(f32[1,128,256]{2,1,0:T(8,128)S(1)} %get-tuple-element.18), channel_id=1, source_target_pairs={{0,1},{1,2},{2,3},{3,4},{4,5},{5,6},{6,7},{7,8},{8,9},{9,10},{10,1... | collective-permute-start | bytes 393224 | tf_op jit(solution)/shard_map/ppermute | solution.py:22
  31.0 9.2 %copy-start.22 = (f32[2,1,128,256]{3,2,1,0:T(8,128)S(1)}, f32[2,1,128,256]{3,2,1,0:T(8,128)}, u32[]{:S(2)}) copy-start(f32[2,1,128,256]{3,2,1,0:T(8,128)} %copy-done.21) | copy-start | bytes 786436
  31.0 9.2 %copy-start.26 = (s32[128,256]{1,0:T(8,128)S(1)}, s32[128,256]{1,0:T(8,128)}, u32[]{:S(2)}) copy-start(s32[128,256]{1,0:T(8,128)} %param.10) | copy-start | bytes 393220
  31.0 8.6 %collective-permute-start.2 = (f32[1,128,256]{2,1,0:T(8,128)S(1)}, f32[1,128,256]{2,1,0:T(8,128)S(1)}, u32[]{:S(2)}, u32[]{:S(2)}) collective-permute-start(f32[1,128,256]{2,1,0:T(8,128)S(1)} %get-tuple-element.19), channel_id=1, source_target_pairs={{1,0},{2,1},{3,2},{4,3},{5,4},{6,5},{7,6},{8,7},{9,8},{10,9},{11,1... | collective-permute-start | bytes 393224 | tf_op jit(solution)/shard_map/ppermute | solution.py:23
  32.5 7.1 %copy-start.17 = (f32[4,127,256]{2,1,0:T(8,128)}, f32[4,127,256]{2,1,0:T(8,128)S(1)}, u32[]{:S(2)}) copy-start(f32[4,127,256]{2,1,0:T(8,128)S(1)} %get-tuple-element.22) | copy-start | bytes 1560580
  32.5 7.1 %copy-start.19 = (f32[4,127,256]{2,1,0:T(8,128)}, f32[4,127,256]{2,1,0:T(8,128)S(1)}, u32[]{:S(2)}) copy-start(f32[4,127,256]{2,1,0:T(8,128)S(1)} %get-tuple-element.23) | copy-start | bytes 1560580
  33.5 6.1 %copy-start.27 = (f32[1,128,256]{2,1,0:T(8,128)}, f32[1,128,256]{2,1,0:T(8,128)S(1)}, u32[]{:S(2)}) copy-start(f32[1,128,256]{2,1,0:T(8,128)S(1)} %collective-permute-done.3) | copy-start | bytes 393220
  39.6 0.6 copy-start.29
  41.4 156.4 %copy-start.31 = (f32[1,8]{1,0:T(1,128)S(1)}, f32[1,8]{1,0:T(1,128)}, u32[]{:S(2)}) copy-start(f32[1,8]{1,0:T(1,128)} %param.11) | copy-start | bytes 100
  198.9 3.8 collective-permute-start.5
  200.2 7.0 %copy-start.2 = (f32[4,128,255]{2,1,0:T(8,128)S(1)}, f32[4,128,255]{2,1,0:T(8,128)}, u32[]{:S(2)}) copy-start(f32[4,128,255]{2,1,0:T(8,128)} %copy-done.1) | copy-start | bytes 1566724
  200.2 7.0 %copy-start.4 = (s32[1,4,128,256]{3,2,1,0:T(8,128)S(1)}, s32[1,4,128,256]{3,2,1,0:T(8,128)}, u32[]{:S(2)}) copy-start(s32[1,4,128,256]{3,2,1,0:T(8,128)} %param.9) | copy-start | bytes 1572868
  200.2 7.0 %copy-start.23 = (f32[2,1,128,256]{3,2,1,0:T(8,128)S(1)}, f32[2,1,128,256]{3,2,1,0:T(8,128)}, u32[]{:S(2)}) copy-start(f32[2,1,128,256]{3,2,1,0:T(8,128)} %copy-done.21) | copy-start | bytes 786436
  200.2 7.0 %collective-permute-start.4 = (f32[1,128,256]{2,1,0:T(8,128)S(1)}, f32[1,128,256]{2,1,0:T(8,128)S(1)}, u32[]{:S(2)}, u32[]{:S(2)}) collective-permute-start(f32[1,128,256]{2,1,0:T(8,128)S(1)} %get-tuple-element.13), channel_id=1, source_target_pairs={{1,0},{2,1},{3,2},{4,3},{5,4},{6,5},{7,6},{8,7},{9,8},{10,9},{11,1... | collective-permute-start | bytes 393224 | tf_op jit(solution)/shard_map/ppermute | solution.py:23
  208.1 8.8 %copy-start.28 = (f32[1,128,256]{2,1,0:T(8,128)S(1)}, f32[1,128,256]{2,1,0:T(8,128)}, u32[]{:S(2)}) copy-start(f32[1,128,256]{2,1,0:T(8,128)} %copy-done.27) | copy-start | bytes 393220
  208.1 8.8 %copy-start.30 = (f32[1,128,256]{2,1,0:T(8,128)S(1)}, f32[1,128,256]{2,1,0:T(8,128)}, u32[]{:S(2)}) copy-start(f32[1,128,256]{2,1,0:T(8,128)} %copy-done.29) | copy-start | bytes 393220
  208.2 8.8 %copy-start.14 = (f32[4,128,255]{2,1,0:T(8,128)S(1)}, f32[4,128,255]{2,1,0:T(8,128)}, u32[]{:S(2)}) copy-start(f32[4,128,255]{2,1,0:T(8,128)} %copy-done.13) | copy-start | bytes 1566724
  208.2 8.8 %copy-start.16 = (f32[4,128,255]{2,1,0:T(8,128)S(1)}, f32[4,128,255]{2,1,0:T(8,128)}, u32[]{:S(2)}) copy-start(f32[4,128,255]{2,1,0:T(8,128)} %copy-done.15) | copy-start | bytes 1566724
  208.2 8.8 %copy-start.18 = (f32[4,127,256]{2,1,0:T(8,128)S(1)}, f32[4,127,256]{2,1,0:T(8,128)}, u32[]{:S(2)}) copy-start(f32[4,127,256]{2,1,0:T(8,128)} %copy-done.17) | copy-start | bytes 1560580
  208.2 8.8 %copy-start.20 = (f32[4,127,256]{2,1,0:T(8,128)S(1)}, f32[4,127,256]{2,1,0:T(8,128)}, u32[]{:S(2)}) copy-start(f32[4,127,256]{2,1,0:T(8,128)} %copy-done.19) | copy-start | bytes 1560580
  208.3 7.0 %collective-permute-start.6 = (f32[1,128,256]{2,1,0:T(8,128)S(1)}, f32[1,128,256]{2,1,0:T(8,128)S(1)}, u32[]{:S(2)}, u32[]{:S(2)}) collective-permute-start(f32[1,128,256]{2,1,0:T(8,128)S(1)} %get-tuple-element.10), channel_id=1, source_target_pairs={{1,0},{2,1},{3,2},{4,3},{5,4},{6,5},{7,6},{8,7},{9,8},{10,9},{11,1... | collective-permute-start | bytes 393224 | tf_op jit(solution)/shard_map/ppermute | solution.py:23
  209.7 7.3 %copy-start.6 = (f32[4,127,256]{2,1,0:T(8,128)S(1)}, f32[4,127,256]{2,1,0:T(8,128)}, u32[]{:S(2)}) copy-start(f32[4,127,256]{2,1,0:T(8,128)} %copy-done.5) | copy-start | bytes 1560580
  209.7 7.3 %copy-start.8 = (f32[4,127,256]{2,1,0:T(8,128)S(1)}, f32[4,127,256]{2,1,0:T(8,128)}, u32[]{:S(2)}) copy-start(f32[4,127,256]{2,1,0:T(8,128)} %copy-done.7) | copy-start | bytes 1560580
  209.7 7.3 %copy-start.10 = (f32[4,128,255]{2,1,0:T(8,128)S(1)}, f32[4,128,255]{2,1,0:T(8,128)}, u32[]{:S(2)}) copy-start(f32[4,128,255]{2,1,0:T(8,128)} %copy-done.9) | copy-start | bytes 1566724
  209.7 7.3 %copy-start.12 = (f32[4,128,255]{2,1,0:T(8,128)S(1)}, f32[4,128,255]{2,1,0:T(8,128)}, u32[]{:S(2)}) copy-start(f32[4,128,255]{2,1,0:T(8,128)} %copy-done.11) | copy-start | bytes 1566724
  209.8 7.2 %collective-permute-start.7 = (f32[1,128,256]{2,1,0:T(8,128)S(1)}, f32[1,128,256]{2,1,0:T(8,128)S(1)}, u32[]{:S(2)}, u32[]{:S(2)}) collective-permute-start(f32[1,128,256]{2,1,0:T(8,128)S(1)} %get-tuple-element.11), channel_id=1, source_target_pairs={{0,1},{1,2},{2,3},{3,4},{4,5},{5,6},{6,7},{7,8},{8,9},{9,10},{10,1... | collective-permute-start | bytes 393224 | tf_op jit(solution)/shard_map/ppermute | solution.py:22
  220.4 251.3 %copy-start.24 = (f32[4,128,256]{2,1,0:T(8,128)S(1)}, f32[4,128,256]{2,1,0:T(8,128)}, u32[]{:S(2)}) copy-start(f32[4,128,256]{2,1,0:T(8,128)} %param.6) | copy-start | bytes 1572868
  292.4 179.3 %copy-start.25 = (f32[4,128,256]{2,1,0:T(8,128)S(1)}, f32[4,128,256]{2,1,0:T(8,128)}, u32[]{:S(2)}) copy-start(f32[4,128,256]{2,1,0:T(8,128)} %all-reduce.22.cloned.1.call-done) | copy-start | bytes 1572868
Sparse Core Ops, SparseCore 0:
  220.5 71.8 all-reduce.21
where the time goes:
time: 480 us; the launch traced here: 479 us
  blocking collectives  333 us (69%)
  waiting for transfers between devices  94.5 us (20%)
  starting transfers between devices  20.1 us (4%)
  between operations  15.9 us (3%)
  other arithmetic  12.7 us (3%)
    psum x1, blocking collectives, shards(): squares = lax.psum(jnp.sum(total * total), 'space')  159 us
    psum x1, blocking collectives, shards(): totals = lax.psum(partial_value, 'space')  156 us
    psum x1, waiting for transfers between devices, shards(): total, misfit = lax.psum((grad_m, misfit_part), 'member')  71.3 us
    psum x1, blocking collectives, shards(): total, misfit = lax.psum((grad_m, misfit_part), 'member')  17.6 us
    ppermute x4, waiting for transfers between devices, extended_2(): after = lax.ppermute(leading, axis, down)  15.7 us
    ppermute x4, starting transfers between devices, extended_2(): before = lax.ppermute(last, axis, up)  14.5 us
  transfers between devices with their start and end apart: 9, of which 9 were waited for; matrix products, arithmetic and copies ran while one was open for 0% of the time, Pallas kernels for 0%

commit v1 on v0

v1 whole, which is shorter than its diff:
```python
import jax
import jax.numpy as jnp
from jax import lax
from jax.experimental import pallas as pl
from jax.experimental.pallas import tpu as pltpu
from jax.sharding import PartitionSpec as P

MESH = pl.DeviceIdType.MESH

NOBS = 8
time_step = 0.015
dissolve_rate = 15.0
descent_rate = 0.5
epsilon = 1e-06

HALF = 0.5 * time_step
RATE = time_step * dissolve_rate
NX, NLO, NZ, NHI = 4, 2, 8, 4
SPACE, MEMBERS = NX * NLO * NZ, 2 * NHI
LAYERS, ROWS, LANES = 4, 128, 256
PAD = 8
SEG = ROWS // NOBS
BLOCK = 32
NB = ROWS // BLOCK


def kernel(
    mean_hbm, pert_hbm, conc_hbm, mask_hbm, ctrl_hbm, obs_ref,
    tot_hbm, row_ref,
    mean, pert, mask, ctrl, K, C, U, D, Pf, Q, L1, X, acc, accq, wgt, dlt,
    g, sib, hsum, rs, tot, lo_buf, xz_buf, y_buf, xz2_buf,
    load_sem, halo_s, halo_r, lo_sem, xz_sem, y_sem, xz2_sem, sib_sem, rs_s, rs_r, ag_s, ag_r, sg_s, sg_r, out_sem,
):
    m, s = lax.axis_index("member"), lax.axis_index("space")
    core, h = lax.rem(m, 2), m // 2
    z, yl, x = lax.rem(s, NZ), lax.rem(s // NZ, NLO), s // (NZ * NLO)

    def dev(member, space):
        return {"member": member, "space": space}

    right, left = lax.rem(s + 1, SPACE), lax.rem(s + SPACE - 1, SPACE)
    sibling = dev(m + 1 - 2 * core, s)
    other_lo = dev(m, x * (NZ * NLO) + (1 - yl) * NZ + z)
    xz_peers = []
    for dx in (2, 1, 3, 0):
        for dz in (4, 3, 5, 2, 6, 1, 7, 0):
            if dx or dz:
                px, pz = lax.rem(x + dx, NX), lax.rem(z + dz, NZ)
                xz_peers.append(dev(m, px * (NZ * NLO) + yl * NZ + pz))
    y_peers = []
    for dh in (2, 1, 3, 0):
        for dl in (0, 1):
            for dc in (0, 1):
                if dh or dl or dc:
                    ph, pc = lax.rem(h + dh, NHI), lax.rem(core + dc, 2)
                    pyl = lax.rem(yl + dl, NLO)
                    y_peers.append(dev(ph * 2 + pc, x * (NZ * NLO) + pyl * NZ + z))
    barrier = pltpu.get_barrier_semaphore()
    greet = [dev(m, right), dev(m, left)] + xz_peers + y_peers
    for peer in greet:
        pl.semaphore_signal(barrier, inc=1, device_id=peer, device_id_type=MESH)

    inside = pl.ds(PAD, ROWS)
    edges = (0, LAYERS - 1)
    loads = {}

    def load(name, index, src, dst):
        loads[name] = pltpu.make_async_copy(src, dst, load_sem.at[index])
        loads[name].start()

    for i, l in enumerate(edges):
        load(("m", l), i, mean_hbm.at[l], mean.at[l])
        load(("p", l), 2 + i, pert_hbm.at[0, l], pert.at[l])
    for i, l in enumerate(edges):
        load(("c", l), 4 + i, conc_hbm.at[0, l], C.at[l + 1, inside])
    mid = pl.ds(1, LAYERS - 2)
    load("ctrl", 6, ctrl_hbm, ctrl)
    load("m", 7, mean_hbm.at[mid], mean.at[mid])
    load("p", 8, pert_hbm.at[0, mid], pert.at[mid])
    load("c", 9, conc_hbm.at[0, mid], C.at[pl.ds(2, LAYERS - 2), inside])
    load("mask", 10, mask_hbm.at[0], mask)

    zero_rows = jnp.zeros((LAYERS + 2, PAD, LANES), jnp.float32)
    for ref in (K, C, U, D, Pf, Q, L1, X):
        ref[:, 0:PAD, :] = zero_rows
        ref[:, PAD + ROWS : 2 * PAD + ROWS, :] = zero_rows
    acc[...] = jnp.zeros_like(acc)
    accq[...] = jnp.zeros_like(accq)

    lane = lax.broadcasted_iota(jnp.int32, (BLOCK, LANES), 1)
    first_lane, last_lane = lane == 0, lane == LANES - 1
    wide = BLOCK + 2 * PAD

    def ext_rows(b):
        return pl.ds(pl.multiple_of(b * BLOCK, BLOCK), wide)

    def mid_rows(b):
        return pl.ds(pl.multiple_of(b * BLOCK + PAD, PAD), BLOCK)

    def own_rows(b):
        return pl.ds(pl.multiple_of(b * BLOCK, BLOCK), BLOCK)

    def centre(ext):
        return ext[PAD : PAD + BLOCK]

    def along_y(ext):
        down, up = pltpu.roll(ext, 1, 0), pltpu.roll(ext, wide - 1, 0)
        return centre(down) + centre(up)

    def along_z(v):
        down, up = pltpu.roll(v, 1, 1), pltpu.roll(v, LANES - 1, 1)
        return jnp.where(first_lane, 0.0, down) + jnp.where(last_lane, 0.0, up)

    def in_plane(ext):
        return along_y(ext) + along_z(centre(ext))

    def blocks(body):
        lax.fori_loop(0, NB, lambda b, c: (body(b), c)[1], 0)

    def exp_layer(l):
        def body(b):
            K[l + 1, mid_rows(b), :] = jnp.exp(mean[l, own_rows(b), :] + pert[l, own_rows(b), :])
        blocks(body)

    def select_layer(e):
        where_x = s * LAYERS + (e - 1)

        def body(b):
            U[e, mid_rows(b), :] = jnp.where(ctrl[own_rows(b), :] == where_x, K[e, mid_rows(b), :], 0.0)
        blocks(body)

    def parity_rows(b):
        row = lax.broadcasted_iota(jnp.int32, (wide, LANES), 0) + (b * BLOCK - PAD)
        return lax.rem((row + SEG * 2) // SEG, 2)

    def cross_layer(e):
        def body(b):
            u, k = U[e, ext_rows(b), :], K[e, ext_rows(b), :]
            row = parity_rows(b)
            mine = centre(row) == 0
            even = jnp.where(row == 0, u, 0.0)
            odd = u - even
            k_mid = centre(k)
            from_odd = k_mid * along_y(odd) + along_y(k * odd)
            from_even = k_mid * along_y(even) + along_y(k * even)
            Q[e, mid_rows(b), :] = HALF * jnp.where(mine, from_odd, from_even)
        blocks(body)

    def transport_layer(e):
        def body(b):
            rows, ext, own = mid_rows(b), ext_rows(b), own_rows(b)
            k_ext, c_ext, u_ext = K[e, ext, :], C[e, ext, :], U[e, ext, :]
            k, c, u = centre(k_ext), centre(c_ext), centre(u_ext)
            k0, k1 = K[e - 1, rows, :], K[e + 1, rows, :]
            c0, c1 = C[e - 1, rows, :], C[e + 1, rows, :]
            u0, u1 = U[e - 1, rows, :], U[e + 1, rows, :]
            diag = 6.0 * k + (k0 + k1) + in_plane(k_ext)
            rate = RATE * mask[e - 1, own, :].astype(jnp.float32)
            flow_c = k * (c0 + c1 + in_plane(c_ext)) + (k0 * c0 + k1 * c1) + in_plane(k_ext * c_ext) - c * diag
            first = c + HALF * flow_c + rate * (1.0 - c)
            flow_u = k * (u0 + u1 + in_plane(u_ext)) + (k0 * u0 + k1 * u1) + in_plane(k_ext * u_ext) - u * diag
            adj = u + HALF * flow_u - rate * u
            D[e, rows, :] = first
            Pf[e, rows, :] = adj
            acc[own, :] += adj * first + u * rate
            accq[own, :] += Q[e, rows, :] * first
        blocks(body)

    for l in edges:
        loads[("m", l)].wait()
        loads[("p", l)].wait()
        exp_layer(l)
    for l in edges:
        loads[("c", l)].wait()
    pl.semaphore_wait(barrier, len(greet))

    def halo(fields, first):
        copies = []
        for i, ref in enumerate(fields):
            for j, (src, dst, to) in enumerate(((LAYERS, 0, right), (1, LAYERS + 1, left))):
                n = first + 2 * i + j
                copies.append(
                    pltpu.make_async_remote_copy(
                        src_ref=ref.at[src, inside], dst_ref=ref.at[dst, inside],
                        send_sem=halo_s.at[n], recv_sem=halo_r.at[n],
                        device_id=dev(m, to), device_id_type=MESH,
                    )
                )
                copies[-1].start()
        return copies

    halo_1 = halo((K, C), 0)
    loads["m"].wait()
    loads["p"].wait()
    exp_layer(1)
    exp_layer(2)
    loads["ctrl"].wait()
    for e in range(1, LAYERS + 1):
        select_layer(e)
    for e in range(1, LAYERS + 1):
        cross_layer(e)
    loads["c"].wait()
    loads["mask"].wait()
    transport_layer(2)
    transport_layer(3)

    def clear(refs):
        blank = jnp.zeros((ROWS, LANES), jnp.float32)

        @pl.when(s == 0)
        def _():
            for ref in refs:
                ref[0, PAD : PAD + ROWS, :] = blank

        @pl.when(s == SPACE - 1)
        def _():
            for ref in refs:
                ref[LAYERS + 1, PAD : PAD + ROWS, :] = blank

    for copy in halo_1:
        copy.wait_recv()
    clear((K, C))
    select_layer(0)
    select_layer(LAYERS + 1)
    transport_layer(1)
    transport_layer(LAYERS)
    halo_2 = halo((D, Pf), 4)

    eye = (lax.broadcasted_iota(jnp.int32, (NOBS, 128), 0) == lax.broadcasted_iota(jnp.int32, (NOBS, 128), 1)).astype(jnp.float32)
    sub = lax.broadcasted_iota(jnp.int32, (NOBS, 128), 0)

    def group(ref, r):
        tile = ref[8 * r : 8 * r + 8, :]
        return tile[:, :128] + tile[:, 128:]

    crosses = [group(accq, r) for r in range(2 * NOBS)]
    parts = jnp.zeros((NOBS, 128), jnp.float32)
    for j in range(NOBS):
        a, b = 2 * j, 2 * j + 1
        tile = group(acc, a) + group(acc, b) - crosses[a] - crosses[b]
        if j > 0:
            tile = tile + crosses[a - 1]
        if j < NOBS - 1:
            tile = tile + crosses[b + 1]
        parts = jnp.where(sub == j, jnp.sum(tile, axis=0, keepdims=True), parts)

    def to_row(column):
        return jnp.sum(eye * column, axis=0, keepdims=True)

    def exchange(buf, slot, row, peers, sems):
        buf[slot] = row
        for peer in peers:
            pltpu.make_async_remote_copy(
                src_ref=buf.at[slot], dst_ref=buf.at[slot],
                send_sem=sems.at[0], recv_sem=sems.at[1],
                device_id=peer, device_id_type=MESH,
            ).start()

    def finish(buf, count, sems):
        span = buf.at[pl.ds(0, count)]
        pltpu.make_async_copy(span, span, sems.at[1]).wait()
        pltpu.make_async_copy(span, span, sems.at[0]).wait()
        return jnp.sum(buf[...], axis=0)

    exchange(lo_buf, yl, to_row(jnp.sum(parts, axis=1, keepdims=True)), [other_lo], lo_sem)
    row = finish(lo_buf, 1, lo_sem)
    exchange(xz_buf, x * NZ + z, row, xz_peers, xz_sem)

    for copy in halo_2:
        copy.wait_recv()
    clear((D, Pf))
    cross_layer(0)
    cross_layer(LAYERS + 1)
    row = finish(xz_buf, NX * NZ - 1, xz_sem)

    observed = jnp.zeros((NOBS, 128), jnp.float32)
    for j in range(NOBS):
        observed = jnp.where(sub == j, obs_ref[0, j], observed)
    total_column = jnp.sum(eye * row, axis=1, keepdims=True)
    resid = total_column * (1.0 / (ROWS * LANES // NOBS)) - observed
    misfit = jnp.sum(resid * resid, axis=0, keepdims=True)
    for r in range(2 * NOBS):
        j = r // 2
        other = max(j - 1, 0) if r % 2 == 0 else min(j + 1, NOBS - 1)
        mine = jnp.broadcast_to(resid[j : j + 1], (8, 128))
        delta = jnp.broadcast_to(resid[other : other + 1], (8, 128)) - mine
        for half in (0, 128):
            wgt[8 * r : 8 * r + 8, half : half + 128] = mine
            dlt[8 * r : 8 * r + 8, half : half + 128] = delta

    def weigh_layer(e):
        def body(b):
            rows, own = mid_rows(b), own_rows(b)
            w = wgt[own, :]
            lam2 = w * U[e, rows, :]
            lam1 = w * Pf[e, rows, :] + dlt[own, :] * Q[e, rows, :]
            U[e, rows, :] = lam2
            L1[e, rows, :] = lam1
            X[e, rows, :] = lam2 * D[e, rows, :] + lam1 * C[e, rows, :]
        blocks(body)

    for e in range(LAYERS + 2):
        weigh_layer(e)

    def gradient_block(e, b):
        rows, ext, own = mid_rows(b), ext_rows(b), own_rows(b)

        def near(ref):
            e_ext = ref[e, ext, :]
            return centre(e_ext), ref[e - 1, rows, :] + ref[e + 1, rows, :] + in_plane(e_ext)

        k_ext, d_ext = K[e, ext, :], D[e, ext, :]
        k0, k1 = K[e - 1, rows, :], K[e + 1, rows, :]
        d0, d1 = D[e - 1, rows, :], D[e + 1, rows, :]
        k, d = centre(k_ext), centre(d_ext)
        diag = 6.0 * k + (k0 + k1) + in_plane(k_ext)
        near_d = d0 + d1 + in_plane(d_ext)
        rate = RATE * mask[e - 1, own, :].astype(jnp.float32)
        flow_d = k * near_d + (k0 * d0 + k1 * d1) + in_plane(k_ext * d_ext) - d * diag
        second = d + HALF * flow_d + rate * (1.0 - d)
        lam2, near_lam2 = near(U)
        lam1, near_lam1 = near(L1)
        c, near_c = near(C)
        both, near_both = near(X)
        bracket = near_both + 6.0 * both - lam2 * near_d - d * near_lam2 - lam1 * near_c - c * near_lam1
        g[e - 1, own, :] = lam2 * second - HALF * k * bracket

    half_rows = ROWS // 2
    half_blocks = NB // 2

    def gradient_half(which):
        def body(i, carry):
            gradient_block(i // half_blocks + 1, which * half_blocks + lax.rem(i, half_blocks))
            return carry

        lax.fori_loop(0, LAYERS * half_blocks, body, 0)

    gradient_half(1 - core)
    sib_copy = pltpu.make_async_remote_copy(
        src_ref=g.at[:, pl.ds(pl.multiple_of((1 - core) * half_rows, half_rows), half_rows), :], dst_ref=sib,
        send_sem=sib_sem.at[0], recv_sem=sib_sem.at[1], device_id=sibling, device_id_type=MESH,
    )
    sib_copy.start()
    gradient_half(core)
    sib_copy.wait_recv()

    piece = half_rows // NHI

    def piece_of(chip):
        return pl.ds(pl.multiple_of(chip * piece, piece), piece)

    def add_cores(chip):
        mine = pl.ds(pl.multiple_of(core * half_rows + chip * piece, piece), piece)
        hsum[:, piece_of(chip), :] = g[:, mine, :] + sib[:, piece_of(chip), :]

    scatter = []
    for i, k in enumerate((2, 1, 3)):
        chip = lax.rem(h + k, NHI)
        add_cores(chip)
        scatter.append(
            pltpu.make_async_remote_copy(
                src_ref=hsum.at[:, piece_of(chip), :], dst_ref=rs.at[i],
                send_sem=rs_s.at[i], recv_sem=rs_r.at[i],
                device_id=dev(chip * 2 + core, s), device_id_type=MESH,
            )
        )
        scatter[-1].start()
    add_cores(h)
    for copy in scatter:
        copy.wait_recv()
    total = hsum[:, piece_of(h), :] + rs[0] + rs[1] + rs[2]

    def final_rows(of_core, chip):
        return pl.ds(pl.multiple_of(of_core * half_rows + chip * piece, piece), piece)

    tot[:, final_rows(core, h), :] = total

    def hand_on(chip, i):
        part = tot.at[:, final_rows(core, chip), :]
        copy = pltpu.make_async_remote_copy(
            src_ref=part, dst_ref=part, send_sem=sg_s.at[i], recv_sem=sg_r.at[i],
            device_id=sibling, device_id_type=MESH,
        )
        copy.start()
        return copy

    gather = []
    mine = tot.at[:, final_rows(core, h), :]
    for i, k in enumerate((2, 1, 3)):
        gather.append(
            pltpu.make_async_remote_copy(
                src_ref=mine, dst_ref=mine, send_sem=ag_s.at[i], recv_sem=ag_r.at[i],
                device_id=dev(lax.rem(h + k, NHI) * 2 + core, s), device_id_type=MESH,
            )
        )
        gather[-1].start()
    handed = [hand_on(h, 0)]

    squares = jnp.sum(jnp.sum(total * total, axis=0), axis=0, keepdims=True)
    squares = jnp.sum(squares, axis=1, keepdims=True)
    lane_row = lax.broadcasted_iota(jnp.int32, (1, 128), 1)
    row = jnp.where(lane_row == 0, squares, jnp.where(lane_row == 1, misfit, 0.0))
    exchange(y_buf, yl * MEMBERS + m, row, y_peers, y_sem)
    row = finish(y_buf, MEMBERS * NLO - 1, y_sem)
    exchange(xz2_buf, x * NZ + z, row, xz_peers, xz2_sem)

    for i, k in ((1, 1), (2, 3), (0, 2)):
        gather[i].wait_recv()
        handed.append(hand_on(lax.rem(h + NHI - k, NHI), i + 1))
    for copy in handed:
        copy.wait_recv()
    out = pltpu.make_async_copy(tot, tot_hbm, out_sem)
    out.start()
    row = finish(xz2_buf, NX * NZ - 1, xz2_sem)
    row_ref[...] = row
    for copy in halo_1 + halo_2 + [sib_copy] + scatter + gather + handed:
        copy.wait_send()
    out.wait()


def shards(mean_logk, perturbation, start_conc, source_mask, control_x, observed):
    slab = (LAYERS, ROWS, LANES)
    tall = (LAYERS + 2, ROWS + 2 * PAD, LANES)
    f32 = jnp.float32
    hbm, dma = pl.BlockSpec(memory_space=pl.ANY), pltpu.SemaphoreType.DMA
    piece = ROWS // MEMBERS
    total, row = pl.pallas_call(
        kernel,
        out_shape=(jax.ShapeDtypeStruct(slab, f32), jax.ShapeDtypeStruct((1, 128), f32)),
        in_specs=[hbm] * 5 + [pl.BlockSpec(memory_space=pltpu.SMEM)],
        out_specs=(hbm, pl.BlockSpec(memory_space=pltpu.VMEM)),
        scratch_shapes=[
            pltpu.VMEM(slab, f32), pltpu.VMEM(slab, f32), pltpu.VMEM(slab, jnp.int32), pltpu.VMEM((ROWS, LANES), jnp.int32),
        ]
        + [pltpu.VMEM(tall, f32)] * 8
        + [pltpu.VMEM((ROWS, LANES), f32)] * 4
        + [
            pltpu.VMEM(slab, f32),
            pltpu.VMEM((LAYERS, ROWS // 2, LANES), f32),
            pltpu.VMEM((LAYERS, ROWS // 2, LANES), f32),
            pltpu.VMEM((NHI - 1, LAYERS, piece, LANES), f32),
            pltpu.VMEM(slab, f32),
            pltpu.VMEM((NLO, 1, 128), f32),
            pltpu.VMEM((NX * NZ, 1, 128), f32),
            pltpu.VMEM((MEMBERS * NLO, 1, 128), f32),
            pltpu.VMEM((NX * NZ, 1, 128), f32),
        ]
        + [dma((n,)) for n in (11, 8, 8, 2, 2, 2, 2, 2, 3, 3, 3, 3, 4, 4)]
        + [dma],
        compiler_params=pltpu.CompilerParams(collective_id=0, has_side_effects=True, vmem_limit_bytes=60 << 20),
    )(mean_logk, perturbation, start_conc, source_mask, control_x, observed)
    cells = SPACE * LAYERS * ROWS * LANES
    squares, misfit = row[0, 0], row[0, 1]
    updated = mean_logk - descent_rate * total * lax.rsqrt(squares / cells + epsilon)
    return updated, misfit * (0.5 / (MEMBERS * NOBS * SPACE))


def solution(mesh):
    in_specs = (
        P("space", None, None),
        P("member", "space", None, None),
        P("member", "space", None, None),
        P("member", "space", None, None),
        P(),
        P("member", None),
    )
    out_specs = (P("space", None, None), P())
    return jax.shard_map(shards, mesh=mesh, in_specs=in_specs, out_specs=out_specs, check_vma=False)
```

time: 480 us -> 72.2 us (0.15)
  the two profiles are of different devices: /device:TPU:32 before, /device:TPU:1 now
where the time goes in v1:
time: 72.2 us; the launch traced here: 71.8 us
  Pallas kernels  65.6 us (91%)
  between operations  3.14 us (4%)
  other arithmetic  1.9 us (3%)
  local copies, waits for them, and re-layouts  1.17 us (2%)
    pallas_call x1, Pallas kernels, shards(): pl.pallas_call(kernel, out_shape=(jax.ShapeDtypeStruct(slab, f32), jax.Sh...  65.6 us
    sub x1, other arithmetic, shards(): mean_logk - descent_rate * total * lax.rsqrt(squares / cells + epsilon)  1.9 us

profile of v1, /device:TPU:1, one launch (start us, length us, event | category | flops | bytes accessed | tf_op | source)
XLA Modules:
  0.0 71.8 jit_solution(14080909303080809677)
XLA Ops:
  0.6 0.0 copy-start
  0.6 65.6 %shard_map.77 = (f32[4,128,256]{2,1,0:T(8,128)}, f32[1,128]{1,0:T(1,128)}) custom-call(f32[4,128,256]{2,1,0:T(8,128)} %mean_hbm.1, f32[1,4,128,256]{3,2,1,0:T(8,128)} %pert_hbm.1, f32[1,4,128,256]{3,2,1,0:T(8,128)} %conc_hbm.1, s32[1,4,128,256]{3,2,1,0:T(8,128)} %mask_hbm.1, s32[128,256]{1,0:T(8,128)} %ctrl_hbm.1, f32[1,8]{1,0:T(1,128)} %obs_ref.1), custom_call_target="tpu_custom_call" | custom-call | tf_op jit(solution)/shard_map/pallas_call | solution.py:427
  66.2 0.0 copy-start.1
  66.2 0.6 copy-done.1
  66.8 0.6 fusion
  68.7 0.0 copy-done
  68.7 1.9 %multiply_subtract_fusion = f32[4,128,256]{2,1,0:T(8,128)} fusion(f32[4,128,256]{2,1,0:T(8,128)S(1)} %copy-done, f32[4,128,256]{2,1,0:T(8,128)} %get-tuple-element.4, f32[]{:T(128)} %bitcast), kind=kLoop, calls=%fused_computation | loop fusion | flops 262144 | bytes 1572868 | tf_op jit(solution)/shard_map/sub | solution.py:454
Async XLA Ops:
  0.6 68.1 %copy-start = (f32[4,128,256]{2,1,0:T(8,128)S(1)}, f32[4,128,256]{2,1,0:T(8,128)}, u32[]{:S(2)}) copy-start(f32[4,128,256]{2,1,0:T(8,128)} %mean_hbm.1) | copy-start | bytes 1572868
  66.2 0.6 copy-start.1

commit v2 on v1

v2 whole, which is shorter than its diff:
```python
import jax
import jax.numpy as jnp
from jax import lax
from jax.experimental import pallas as pl
from jax.experimental.pallas import tpu as pltpu
from jax.sharding import PartitionSpec as P

MESH = pl.DeviceIdType.MESH

NOBS = 8
time_step = 0.015
dissolve_rate = 15.0
descent_rate = 0.5
epsilon = 1e-06

HALF = 0.5 * time_step
RATE = time_step * dissolve_rate
NX, NLO, NZ, NHI = 4, 2, 8, 4
SPACE, MEMBERS = NX * NLO * NZ, 2 * NHI
LAYERS, ROWS, LANES = 4, 128, 256
PAD = 8
SEG = ROWS // NOBS
BLOCK = 32
NB = ROWS // BLOCK


def kernel(
    mean_hbm, pert_hbm, conc_hbm, mask_hbm, ctrl_hbm, obs_hbm,
    tot_ref, row_ref,
    mean, pert, mask, ctrl, obs_ref, K, C, U, D, Pf, Dp, G, acc, bnd,
    sib, hsum, rs, tot, lo_buf, xz_buf, y_buf, xz2_buf,
    load_sem, halo_s, halo_r, lo_sem, xz_sem, y_sem, xz2_sem, sib_s, sib_r, rs_s, rs_r, ag_s, ag_r, sg_s, sg_r, out_sem,
):
    m, s = lax.axis_index("member"), lax.axis_index("space")
    core, h = lax.rem(m, 2), m // 2
    z, yl, x = lax.rem(s, NZ), lax.rem(s // NZ, NLO), s // (NZ * NLO)

    def dev(member, space):
        return {"member": member, "space": space}

    right, left = lax.rem(s + 1, SPACE), lax.rem(s + SPACE - 1, SPACE)
    sibling = dev(m + 1 - 2 * core, s)
    other_lo = dev(m, x * (NZ * NLO) + (1 - yl) * NZ + z)
    xz_peers, xzc_peers = [], []
    for dx in (2, 1, 3, 0):
        for dz in (4, 3, 5, 2, 6, 1, 7, 0):
            px, pz = lax.rem(x + dx, NX), lax.rem(z + dz, NZ)
            there = px * (NZ * NLO) + yl * NZ + pz
            if dx or dz:
                xz_peers.append(dev(m, there))
            xzc_peers.append(dev(m + 1 - 2 * core, there))
    xzc_peers += xz_peers
    y_peers = []
    for dh in (2, 1, 3, 0):
        for dl in (0, 1):
            if dh or dl:
                y_peers.append(dev(lax.rem(h + dh, NHI) * 2 + core, x * (NZ * NLO) + lax.rem(yl + dl, NLO) * NZ + z))
    barrier = pltpu.get_barrier_semaphore()
    greet = [dev(m, right), dev(m, left)] + xzc_peers + y_peers
    for peer in greet:
        pl.semaphore_signal(barrier, inc=1, device_id=peer, device_id_type=MESH)

    inside = pl.ds(PAD, ROWS)
    edges = (0, LAYERS - 1)
    loads = {}

    def load(name, index, src, dst):
        loads[name] = pltpu.make_async_copy(src, dst, load_sem.at[index])
        loads[name].start()

    for i, l in enumerate(edges):
        load(("m", l), i, mean_hbm.at[l], mean.at[l])
        load(("p", l), 2 + i, pert_hbm.at[0, l], pert.at[l])
    halves = (pl.ds(0, 128), pl.ds(128, 128))
    for i, l in enumerate(edges):
        for k, lanes in enumerate(halves):
            load(("c", l, k), 4 + 2 * i + k, conc_hbm.at[0, l, :, lanes], C.at[l + 1, k, inside])
    mid = pl.ds(1, LAYERS - 2)
    load("ctrl", 8, ctrl_hbm, ctrl)
    load("m", 9, mean_hbm.at[mid], mean.at[mid])
    load("p", 10, pert_hbm.at[0, mid], pert.at[mid])
    for k, lanes in enumerate(halves):
        load(("c", k), 11 + k, conc_hbm.at[0, mid, :, lanes], C.at[pl.ds(2, LAYERS - 2), k, inside])
    load("mask", 13, mask_hbm.at[0], mask)
    load("obs", 14, obs_hbm, obs_ref)

    zero_rows = jnp.zeros((2, PAD, 128), jnp.float32)
    for ref in (K, C, U, D, Pf):
        for e in range(LAYERS + 2):
            ref[e, :, 0:PAD, :] = zero_rows
            ref[e, :, PAD + ROWS : 2 * PAD + ROWS, :] = zero_rows
    acc[...] = jnp.zeros_like(acc)

    def own_rows(b):
        return pl.ds(pl.multiple_of(b * BLOCK, BLOCK), BLOCK)

    def at(ref, e, b, shift=0):
        start = pl.multiple_of(b * BLOCK, BLOCK) + (PAD + shift)
        return ref[e, :, pl.ds(start, BLOCK), :]

    def put(ref, e, b, value):
        ref[e, :, pl.ds(pl.multiple_of(b * BLOCK + PAD, PAD), BLOCK), :] = value

    def split(v):
        return jnp.stack([v[:, :128], v[:, 128:]])

    def shifts_z(v):
        lane = lax.broadcasted_iota(jnp.int32, v.shape, 2)
        before, after = pltpu.roll(v, 1, 2), pltpu.roll(v, 127, 2)
        zero = jnp.zeros_like(v[0])
        down = jnp.where(lane == 0, jnp.stack([zero, before[0]]), before)
        up = jnp.where(lane == 127, jnp.stack([after[1], zero]), after)
        return down, up

    def neighbours(ref, e, b, beside):
        v = at(ref, e, b)
        return v, [at(ref, n, b) for n in beside] + [at(ref, e, b, -1), at(ref, e, b, 1), *shifts_z(v)]

    def each(layers, body):
        first, step, count = layers

        def run(i, carry):
            body(first + step * (i // NB), lax.rem(i, NB))
            return carry

        lax.fori_loop(0, count * NB, run, 0)

    OUTER, INNER, OWN = (1, LAYERS - 1, 2), (2, 1, LAYERS - 2), (1, 1, LAYERS)

    def conductivity(e, b):
        put(K, e, b, split(jnp.exp(mean[e - 1, own_rows(b), :] + pert[e - 1, own_rows(b), :])))

    def selected(e, b):
        where_x = s * LAYERS + (e - 1)
        put(U, e, b, jnp.where(split(ctrl[own_rows(b), :]) == where_x, at(K, e, b), 0.0))

    def edge_of(e):
        return (e - 1) // (LAYERS - 1)

    def inner_of(e):
        return 2 + edge_of(e) * (LAYERS - 3), edge_of(e) * (LAYERS + 1)

    def rate_of(e, b):
        return RATE * split(mask[e - 1, own_rows(b), :]).astype(jnp.float32)

    def gather_discharge(e, b, first, adj, u):
        acc[:, own_rows(b), :] += adj * first + u * rate_of(e, b)

    def transport_block(e, b, beside):
        k, ks = neighbours(K, e, b, beside)
        c, cs = neighbours(C, e, b, beside)
        u, us = neighbours(U, e, b, beside)
        flow_c, flow_u = jnp.zeros_like(c), jnp.zeros_like(u)
        for kn, cn, un in zip(ks, cs, us):
            face = k + kn
            flow_c, flow_u = flow_c + face * (cn - c), flow_u + face * (un - u)
        rate = rate_of(e, b)
        first = c + HALF * flow_c + rate * (1.0 - c)
        adj = u + HALF * flow_u - rate * u
        put(Pf, e, b, adj)
        return first, adj, u

    def transport_inner(e, b):
        first, adj, u = transport_block(e, b, (e - 1, e + 1))
        put(D, e, b, first)
        gather_discharge(e, b, first, adj, u)

    def transport_outer(e, b):
        Dp[edge_of(e), :, own_rows(b), :] = transport_block(e, b, (inner_of(e)[0],))[0]

    def transport_halo(e, b):
        n = inner_of(e)[1]
        face = HALF * (at(K, e, b) + at(K, n, b))
        u = at(U, e, b)
        first = Dp[edge_of(e), :, own_rows(b), :] + face * (at(C, n, b) - at(C, e, b))
        adj = at(Pf, e, b) + face * (at(U, n, b) - u)
        put(D, e, b, first)
        put(Pf, e, b, adj)
        gather_discharge(e, b, first, adj, u)

    def gradient_block(e, b, beside):
        fields = [neighbours(ref, e, b, beside) for ref in (K, C, U, D, Pf)]
        k, c, u, d, p = (centre for centre, _ in fields)
        flow_d, bracket = jnp.zeros_like(d), jnp.zeros_like(d)
        for kn, cn, un, dn, pn in zip(*(around for _, around in fields)):
            slope = dn - d
            flow_d = flow_d + (k + kn) * slope
            bracket = bracket + ((un - u) * slope + (pn - p) * (cn - c))
        second = d + HALF * flow_d + rate_of(e, b) * (1.0 - d)
        G[e - 1, :, own_rows(b), :] = u * second - HALF * k * bracket

    def gradient_inner(e, b):
        gradient_block(e, b, (e - 1, e + 1))

    def gradient_outer(e, b):
        gradient_block(e, b, (inner_of(e)[0],))

    def gradient_halo(e, b):
        n, own = inner_of(e)[1], own_rows(b)
        k, kn, u, un = at(K, e, b), at(K, n, b), at(U, e, b), at(U, n, b)
        slope = at(C, n, b) - at(C, e, b)
        inside_grid = jnp.where(s == edge_of(e) * (SPACE - 1), 0.0, 1.0)
        dn = (at(D, n, b) - HALF * (k + kn) * slope) * inside_grid
        by_d = (dn - at(D, e, b)) * (u * (k + kn) - k * (un - u))
        by_c = k * (at(Pf, n, b) * inside_grid - at(Pf, e, b)) * slope
        G[e - 1, :, own, :] += HALF * (by_d - by_c)

    SIDES = ((0, -1, 1), (SEG - 1, SEG, SEG - 2))

    def strided(ref, e, row):
        return ref[e, :, pl.ds(PAD + row, NOBS, stride=SEG), :]

    def crossing(e, side):
        own_row, over, _ = side
        return HALF * (strided(K, e, own_row) + strided(K, e, over)) * strided(U, e, over)

    def crossing_terms(e):
        return [crossing(e, side) * strided(D, e, side[0]) for side in SIDES]

    def boundary_gradient(e):
        for i, side in enumerate(SIDES):
            row, over, further = side
            q, k, c = crossing(e, side), strided(K, e, row), strided(C, e, row)
            u_over, c_over, c_further = strided(U, e, over), strided(C, e, over), strided(C, e, further)
            p_over = strided(Pf, e, over) - HALF * (k + strided(K, e, over)) * strided(U, e, row)
            bracket = u_over * (strided(D, e, over) - strided(D, e, row))
            bracket += (p_over - q) * (c_over - c) - q * (c_further - c)
            for n in (e - 1, e + 1):
                bracket += (crossing(n, side) - q) * (strided(C, n, row) - c)
            for qn, cn in zip(shifts_z(q), shifts_z(c)):
                bracket += (qn - q) * (cn - c)
            bnd[e - 1, 2 * i] = -HALF * k * bracket
            bnd[e - 1, 2 * i + 1] = -HALF * strided(K, e, further) * (q * (c - c_further))

    for l in edges:
        loads[("m", l)].wait()
        loads[("p", l)].wait()
    each(OUTER, conductivity)
    for l in edges:
        for k in (0, 1):
            loads[("c", l, k)].wait()
    pl.semaphore_wait(barrier, len(greet))

    def halo(pairs, first):
        copies = []
        for i, (low, high, at_left, at_right) in enumerate(pairs):
            for j, (src, dst, to) in enumerate(((high, at_right, right), (low, at_left, left))):
                n = first + 2 * i + j
                copies.append(
                    pltpu.make_async_remote_copy(
                        src_ref=src, dst_ref=dst, send_sem=halo_s.at[n], recv_sem=halo_r.at[n],
                        device_id=dev(m, to), device_id_type=MESH,
                    )
                )
                copies[-1].start()
        return copies

    def layers_of(ref):
        return tuple(ref.at[e, :, inside] for e in (1, LAYERS, LAYERS + 1, 0))

    halo_1 = halo((layers_of(K), layers_of(C)), 0)
    loads["m"].wait()
    loads["p"].wait()
    each(INNER, conductivity)
    loads["ctrl"].wait()
    each(OWN, selected)
    for k in (0, 1):
        loads[("c", k)].wait()
    loads["mask"].wait()
    loads["obs"].wait()
    each(OUTER, transport_outer)
    halo_2 = halo(((Dp.at[0], Dp.at[1], *layers_of(D)[2:]),), 4)
    each(INNER, transport_inner)
    cross_in = [crossing_terms(e) for e in range(2, LAYERS)]

    def clear(refs):
        blank = jnp.zeros((2, ROWS, 128), jnp.float32)

        @pl.when(s == 0)
        def _():
            for ref in refs:
                ref[0, :, PAD : PAD + ROWS, :] = blank

        @pl.when(s == SPACE - 1)
        def _():
            for ref in refs:
                ref[LAYERS + 1, :, PAD : PAD + ROWS, :] = blank

    for copy in halo_1:
        copy.wait_recv()
    clear((K, C))
    each((0, LAYERS + 1, 2), selected)
    each(OUTER, transport_halo)

    eye = (lax.broadcasted_iota(jnp.int32, (NOBS, 128), 0) == lax.broadcasted_iota(jnp.int32, (NOBS, 128), 1)).astype(jnp.float32)
    sub = lax.broadcasted_iota(jnp.int32, (NOBS, 128), 0)
    parts = acc[:, pl.ds(0, NOBS, stride=SEG), :]
    for i in range(1, SEG):
        parts = parts + acc[:, pl.ds(i, NOBS, stride=SEG), :]
    cross_all = cross_in + [crossing_terms(1), crossing_terms(LAYERS)]
    lower, upper = (sum(terms[i] for terms in cross_all) for i in (0, 1))
    parts = parts - lower - upper + pltpu.roll(lower, NOBS - 1, 1) + pltpu.roll(upper, 1, 1)
    column = jnp.sum(parts[0] + parts[1], axis=1, keepdims=True)

    def to_row(column):
        return jnp.sum(eye * column, axis=0, keepdims=True)

    def exchange(buf, slot, row, peers, sems):
        buf[slot] = row
        for peer in peers:
            pltpu.make_async_remote_copy(
                src_ref=buf.at[slot], dst_ref=buf.at[slot],
                send_sem=sems.at[0], recv_sem=sems.at[1],
                device_id=peer, device_id_type=MESH,
            ).start()

    def finish(buf, count, sems):
        span = buf.at[pl.ds(0, count)]
        pltpu.make_async_copy(span, span, sems.at[1]).wait()
        pltpu.make_async_copy(span, span, sems.at[0]).wait()
        return jnp.sum(buf[...], axis=0)

    exchange(lo_buf, yl, to_row(column), [other_lo], lo_sem)
    row = finish(lo_buf, 1, lo_sem)
    exchange(xz_buf, x * NZ + z, row, xz_peers, xz_sem)
    halo_2 += halo((layers_of(Pf),), 6)

    each(INNER, gradient_inner)
    each(OUTER, gradient_outer)
    for e in range(2, LAYERS):
        boundary_gradient(e)
    for copy in halo_2:
        copy.wait_recv()
    each(OUTER, gradient_halo)
    boundary_gradient(1)
    boundary_gradient(LAYERS)
    row = finish(xz_buf, NX * NZ - 1, xz_sem)

    observed = jnp.zeros((NOBS, 128), jnp.float32)
    for j in range(NOBS):
        observed = jnp.where(sub == j, obs_ref[0, j], observed)
    total_column = jnp.sum(eye * row, axis=1, keepdims=True)
    resid = total_column * (1.0 / (ROWS * LANES // NOBS)) - observed
    misfit = jnp.sum(resid * resid, axis=0, keepdims=True)
    below = jnp.where(sub == 0, 0.0, pltpu.roll(resid, 1, 0) - resid)
    above = jnp.where(sub == NOBS - 1, 0.0, pltpu.roll(resid, NOBS - 1, 0) - resid)
    deltas = (below, above)

    def weigh(l, carry):
        for half in (0, 1):
            for j in range(NOBS):
                rows = pl.ds(j * SEG, SEG)
                G[l, half, rows, :] = G[l, half, rows, :] * jnp.broadcast_to(resid[j : j + 1], (SEG, 128))
            for i, (row, _, further) in enumerate(SIDES):
                for k, r in enumerate((row, further)):
                    where = pl.ds(r, NOBS, stride=SEG)
                    G[l, half, where, :] = G[l, half, where, :] + deltas[i] * bnd[l, 2 * i + k, half]
        return carry

    lax.fori_loop(0, LAYERS, weigh, 0)

    half_rows = ROWS // 2
    piece = half_rows // NHI

    def piece_of(chip):
        return pl.ds(pl.multiple_of(chip * piece, piece), piece)

    def rows_of(of_core, chip):
        return pl.ds(pl.multiple_of(of_core * half_rows + chip * piece, piece), piece)

    order = (2, 1, 3, 0)
    cores = []
    for i, k in enumerate(order):
        chip = lax.rem(h + k, NHI)
        cores.append(
            pltpu.make_async_remote_copy(
                src_ref=G.at[:, :, rows_of(1 - core, chip), :], dst_ref=sib.at[:, :, piece_of(chip), :],
                send_sem=sib_s.at[i], recv_sem=sib_r.at[i], device_id=sibling, device_id_type=MESH,
            )
        )
        cores[-1].start()
    scatter = []
    for i, k in enumerate(order):
        chip = lax.rem(h + k, NHI)
        cores[i].wait_recv()
        hsum[:, :, piece_of(chip), :] = G[:, :, rows_of(core, chip), :] + sib[:, :, piece_of(chip), :]
        if k:
            scatter.append(
                pltpu.make_async_remote_copy(
                    src_ref=hsum.at[:, :, piece_of(chip), :], dst_ref=rs.at[i],
                    send_sem=rs_s.at[i], recv_sem=rs_r.at[i],
                    device_id=dev(chip * 2 + core, s), device_id_type=MESH,
                )
            )
            scatter[-1].start()
    for copy in scatter:
        copy.wait_recv()
    total = hsum[:, :, piece_of(h), :] + rs[0] + rs[1] + rs[2]
    tot[:, :, rows_of(core, h), :] = total

    def hand_on(chip, i):
        part = tot.at[:, :, rows_of(core, chip), :]
        copy = pltpu.make_async_remote_copy(
            src_ref=part, dst_ref=part, send_sem=sg_s.at[i], recv_sem=sg_r.at[i],
            device_id=sibling, device_id_type=MESH,
        )
        copy.start()
        return copy

    gather = []
    mine = tot.at[:, :, rows_of(core, h), :]
    for i, k in enumerate((2, 1, 3)):
        gather.append(
            pltpu.make_async_remote_copy(
                src_ref=mine, dst_ref=mine, send_sem=ag_s.at[i], recv_sem=ag_r.at[i],
                device_id=dev(lax.rem(h + k, NHI) * 2 + core, s), device_id_type=MESH,
            )
        )
        gather[-1].start()
    handed = [hand_on(h, 0)]

    squares = jnp.sum(jnp.sum(total * total, axis=(0, 1)), axis=0, keepdims=True)
    squares = jnp.sum(squares, axis=1, keepdims=True)
    lane_row = lax.broadcasted_iota(jnp.int32, (1, 128), 1)
    row = jnp.where(lane_row == 0, squares, jnp.where(lane_row == 1, misfit, 0.0))
    exchange(xz2_buf, (x * NZ + z) * 2 + core, row, xzc_peers, xz2_sem)
    row = finish(xz2_buf, 2 * NX * NZ - 1, xz2_sem)
    exchange(y_buf, h * NLO + yl, row, y_peers, y_sem)

    for i, k in ((1, 1), (2, 3), (0, 2)):
        gather[i].wait_recv()
        handed.append(hand_on(lax.rem(h + NHI - k, NHI), i + 1))
    for copy in handed:
        copy.wait_recv()
    out = pltpu.make_async_copy(tot, tot_ref, out_sem)
    out.start()
    for copy in halo_1 + halo_2 + cores + scatter + gather + handed:
        copy.wait_send()
    row = finish(y_buf, NHI * NLO - 1, y_sem)
    row_ref[...] = row
    out.wait()


def update_kernel(row_ref, mean_ref, tot_ref, out_ref, misfit_ref):
    squares = jnp.full((8, 128), row_ref[0, 0])
    scale = descent_rate * lax.rsqrt(squares * (1.0 / (SPACE * LAYERS * ROWS * LANES)) + epsilon)
    for l in range(LAYERS):
        for r in range(0, ROWS, 8):
            for k in (0, 1):
                lanes = slice(128 * k, 128 * k + 128)
                out_ref[l, r : r + 8, lanes] = mean_ref[l, r : r + 8, lanes] - scale * tot_ref[l, k, r : r + 8, :]
    misfit_ref[0, 0] = row_ref[0, 1] * (0.5 / (MEMBERS * NOBS * SPACE))


def shards(mean_logk, perturbation, start_conc, source_mask, control_x, observed):
    slab = (LAYERS, ROWS, LANES)
    halved = (LAYERS, 2, ROWS, 128)
    tall = (LAYERS + 2, 2, ROWS + 2 * PAD, 128)
    f32 = jnp.float32
    dma = pltpu.SemaphoreType.DMA
    hbm, anywhere = pl.BlockSpec(memory_space=pltpu.HBM), pl.BlockSpec(memory_space=pl.ANY)
    vmem, smem = pl.BlockSpec(memory_space=pltpu.VMEM), pl.BlockSpec(memory_space=pltpu.SMEM)
    piece = ROWS // MEMBERS
    pinned = [
        pltpu.with_memory_space_constraint(v, pltpu.HBM) for v in (mean_logk, perturbation, start_conc, source_mask, control_x, observed)
    ]
    total, row = pl.pallas_call(
        kernel,
        out_shape=(jax.ShapeDtypeStruct(halved, f32), jax.ShapeDtypeStruct((1, 128), f32)),
        in_specs=[hbm] * 6,
        out_specs=(anywhere, vmem),
        scratch_shapes=[
            pltpu.VMEM(slab, f32), pltpu.VMEM(slab, f32), pltpu.VMEM(slab, jnp.int32), pltpu.VMEM((ROWS, LANES), jnp.int32),
            pltpu.SMEM((1, NOBS), f32),
        ]
        + [pltpu.VMEM(tall, f32)] * 5
        + [
            pltpu.VMEM((2, 2, ROWS, 128), f32),
            pltpu.VMEM(halved, f32),
            pltpu.VMEM((2, ROWS, 128), f32),
            pltpu.VMEM((LAYERS, 4, 2, NOBS, 128), f32),
            pltpu.VMEM((LAYERS, 2, ROWS // 2, 128), f32),
            pltpu.VMEM((LAYERS, 2, ROWS // 2, 128), f32),
            pltpu.VMEM((NHI - 1, LAYERS, 2, piece, 128), f32),
            pltpu.VMEM(halved, f32),
            pltpu.VMEM((NLO, 1, 128), f32),
            pltpu.VMEM((NX * NZ, 1, 128), f32),
            pltpu.VMEM((NHI * NLO, 1, 128), f32),
            pltpu.VMEM((2 * NX * NZ, 1, 128), f32),
        ]
        + [dma((n,)) for n in (15, 8, 8, 2, 2, 2, 2, 4, 4, 3, 3, 3, 3, 4, 4)]
        + [dma],
        compiler_params=pltpu.CompilerParams(collective_id=0, has_side_effects=True, vmem_limit_bytes=24 << 20),
        name="step",
    )(*pinned)
    updated, misfit = pl.pallas_call(
        update_kernel,
        out_shape=(jax.ShapeDtypeStruct(slab, f32), jax.ShapeDtypeStruct((1, 1), f32)),
        in_specs=[smem, vmem, vmem],
        out_specs=(vmem, smem),
        compiler_params=pltpu.CompilerParams(vmem_limit_bytes=8 << 20),
        name="update",
    )(row, mean_logk, total)
    return updated, misfit[0, 0]


def solution(mesh):
    in_specs = (
        P("space", None, None),
        P("member", "space", None, None),
        P("member", "space", None, None),
        P("member", "space", None, None),
        P(),
        P("member", None),
    )
    out_specs = (P("space", None, None), P())
    return jax.shard_map(shards, mesh=mesh, in_specs=in_specs, out_specs=out_specs, check_vma=False)
```

time: 72.2 us -> 55.8 us (0.77)
  Pallas kernels: 65.6 us -> 55 us
  between operations: 3.14 us -> 0.66 us
  other arithmetic: 1.9 us -> 0 us
  local copies, waits for them, and re-layouts: 1.17 us -> 0.01 us
    pallas_call x1 -> x2, Pallas kernels: 65.6 us -> 55 us  [the longest x1 53.6 us: shards(): pl.pallas_call(kernel, out_shape=(jax.ShapeDtypeStruct(halved, f32), jax....]
    sub x1 -> x0, other arithmetic: 1.9 us -> none  [shards(): mean_logk - descent_rate * total * lax.rsqrt(squares / cells + epsilon)]
where the time goes in v2:
time: 55.8 us; the launch traced here: 55.7 us
  Pallas kernels  55 us (99%)
  between operations  0.66 us (1%)
    pallas_call x1, Pallas kernels, shards(): pl.pallas_call(kernel, out_shape=(jax.ShapeDtypeStruct(halved, f32), jax....  53.6 us
    pallas_call x1, Pallas kernels, shards(): pl.pallas_call(update_kernel, out_shape=(jax.ShapeDtypeStruct(slab, f32),...  1.42 us

profile of v2, /device:TPU:1, one launch (start us, length us, event | category | flops | bytes accessed | tf_op | source)
XLA Modules:
  0.0 55.7 jit_solution(1018412616785329684)
XLA Ops:
  0.6 0.0 copy-start
  0.6 53.6 %step.1 = (f32[4,2,128,128]{3,2,1,0:T(8,128)S(1)}, f32[1,128]{1,0:T(1,128)S(1)}) custom-call(f32[4,128,256]{2,1,0:T(8,128)} %mean_ref.1, f32[1,4,128,256]{3,2,1,0:T(8,128)} %pert_hbm.1, f32[1,4,128,256]{3,2,1,0:T(8,128)} %conc_hbm.1, s32[1,4,128,256]{3,2,1,0:T(8,128)} %mask_hbm.1, s32[128,256]{1,0:T(8,128)} %ctrl_hbm.1, f32[1,8]{1,0:T(1,128)} %obs_hbm.1), custom_call_target="tpu_custom_call" | custom-call | tf_op jit(solution)/shard_map/step/pallas_call | solution.py:467
  54.3 0.0 copy-done
  54.3 1.4 %update.1 = (f32[4,128,256]{2,1,0:T(8,128)}, f32[1,1]{1,0:T(1,128)}) custom-call(f32[1,128]{1,0:T(1,128)S(1)} %get-tuple-element.6.row_ref, f32[4,128,256]{2,1,0:T(8,128)S(1)} %copy-done, f32[4,2,128,128]{3,2,1,0:T(8,128)S(1)} %get-tuple-element.7.tot_ref), custom_call_target="tpu_custom_call" | custom-call | tf_op jit(solution)/shard_map/update/pallas_call | solution.py:496
Async XLA Ops:
  0.6 53.6 %copy-start = (f32[4,128,256]{2,1,0:T(8,128)S(1)}, f32[4,128,256]{2,1,0:T(8,128)}, u32[]{:S(2)}) copy-start(f32[4,128,256]{2,1,0:T(8,128)} %mean_ref.1) | copy-start | bytes 1572868

commit v3 on v2

--- a/solution.py
+++ b/solution.py
@@ -28,8 +28,8 @@
     mean_hbm, pert_hbm, conc_hbm, mask_hbm, ctrl_hbm, obs_hbm,
     tot_ref, row_ref,
     mean, pert, mask, ctrl, obs_ref, K, C, U, D, Pf, Dp, G, acc, bnd,
-    sib, hsum, rs, tot, lo_buf, xz_buf, y_buf, xz2_buf,
-    load_sem, halo_s, halo_r, lo_sem, xz_sem, y_sem, xz2_sem, sib_s, sib_r, rs_s, rs_r, ag_s, ag_r, sg_s, sg_r, out_sem,
+    sib, hsum, rs, tot, space_buf, y_buf, plane_buf,
+    load_sem, halo_s, halo_r, space_sem, y_sem, plane_sem, sib_s, sib_r, rs_s, rs_r, ag_s, ag_r, sg_s, sg_r, out_sem, relay,
 ):
     m, s = lax.axis_index("member"), lax.axis_index("space")
     core, h = lax.rem(m, 2), m // 2
@@ -40,25 +40,28 @@
 
     right, left = lax.rem(s + 1, SPACE), lax.rem(s + SPACE - 1, SPACE)
     sibling = dev(m + 1 - 2 * core, s)
-    other_lo = dev(m, x * (NZ * NLO) + (1 - yl) * NZ + z)
-    xz_peers, xzc_peers = [], []
-    for dx in (2, 1, 3, 0):
-        for dz in (4, 3, 5, 2, 6, 1, 7, 0):
-            px, pz = lax.rem(x + dx, NX), lax.rem(z + dz, NZ)
-            there = px * (NZ * NLO) + yl * NZ + pz
-            if dx or dz:
-                xz_peers.append(dev(m, there))
-            xzc_peers.append(dev(m + 1 - 2 * core, there))
-    xzc_peers += xz_peers
-    y_peers = []
-    for dh in (2, 1, 3, 0):
-        for dl in (0, 1):
-            if dh or dl:
-                y_peers.append(dev(lax.rem(h + dh, NHI) * 2 + core, x * (NZ * NLO) + lax.rem(yl + dl, NLO) * NZ + z))
+
+    def place(dx, dl, dz):
+        return (lax.rem(x + dx, NX) * NLO + lax.rem(yl + dl, NLO)) * NZ + lax.rem(z + dz, NZ)
+
+    far_x, far_z, far_h = (2, 1, 3, 0), (4, 3, 5, 2, 6, 1, 7, 0), (2, 1, 3, 0)
+    plane = [(dx, dz) for dx in far_x for dz in far_z]
+    space_peers = [dev(m, place(dx, dl, dz)) for dx, dz in plane for dl in (1, 0) if dx or dl or dz]
+    plane_peers = [dev(m + 1 - 2 * core, place(dx, 0, dz)) for dx, dz in plane]
+    plane_peers += [dev(m, place(dx, 0, dz)) for dx, dz in plane if dx or dz]
+    y_peers = [dev(lax.rem(h + dh, NHI) * 2 + core, place(0, dl, 0)) for dh in far_h for dl in (1, 0) if dh or dl]
+
+    def greet(semaphore, peers):
+        for peer in peers:
+            pl.semaphore_signal(semaphore, inc=1, device_id=peer, device_id_type=MESH)
+
+    z_ring = [dev(m, place(0, 0, dz)) for dz in far_z if dz]
+    x_ring = [dev(m, place(dx, 0, 0)) for dx in far_x if dx]
+    h_near = [dev(lax.rem(h + dh, NHI) * 2 + core, s) for dh in (1, NHI - 1)]
+    beside = [dev(m, place(0, 1, 0)), sibling]
+    near = [dev(m, right), dev(m, left)] + z_ring + x_ring + h_near + beside
     barrier = pltpu.get_barrier_semaphore()
-    greet = [dev(m, right), dev(m, left)] + xzc_peers + y_peers
-    for peer in greet:
-        pl.semaphore_signal(barrier, inc=1, device_id=peer, device_id_type=MESH)
+    greet(barrier, near)
 
     inside = pl.ds(PAD, ROWS)
     edges = (0, LAYERS - 1)
@@ -239,7 +242,8 @@
     for l in edges:
         for k in (0, 1):
             loads[("c", l, k)].wait()
-    pl.semaphore_wait(barrier, len(greet))
+    pl.semaphore_wait(barrier, len(near))
+    greet(relay.at[0], x_ring + h_near)
 
     def halo(pairs, first):
         copies = []
@@ -262,6 +266,8 @@
     loads["m"].wait()
     loads["p"].wait()
     each(INNER, conductivity)
+    pl.semaphore_wait(relay.at[0], len(x_ring + h_near))
+    greet(relay.at[1], beside)
     loads["ctrl"].wait()
     each(OWN, selected)
     for k in (0, 1):
@@ -320,9 +326,8 @@
         pltpu.make_async_copy(span, span, sems.at[0]).wait()
         return jnp.sum(buf[...], axis=0)
 
-    exchange(lo_buf, yl, to_row(column), [other_lo], lo_sem)
-    row = finish(lo_buf, 1, lo_sem)
-    exchange(xz_buf, x * NZ + z, row, xz_peers, xz_sem)
+    pl.semaphore_wait(relay.at[1], len(beside))
+    exchange(space_buf, s, to_row(column), space_peers, space_sem)
     halo_2 += halo((layers_of(Pf),), 6)
 
     each(INNER, gradient_inner)
@@ -334,7 +339,7 @@
     each(OUTER, gradient_halo)
     boundary_gradient(1)
     boundary_gradient(LAYERS)
-    row = finish(xz_buf, NX * NZ - 1, xz_sem)
+    row = finish(space_buf, SPACE - 1, space_sem)
 
     observed = jnp.zeros((NOBS, 128), jnp.float32)
     for j in range(NOBS):
@@ -423,8 +428,8 @@
     squares = jnp.sum(squares, axis=1, keepdims=True)
     lane_row = lax.broadcasted_iota(jnp.int32, (1, 128), 1)
     row = jnp.where(lane_row == 0, squares, jnp.where(lane_row == 1, misfit, 0.0))
-    exchange(xz2_buf, (x * NZ + z) * 2 + core, row, xzc_peers, xz2_sem)
-    row = finish(xz2_buf, 2 * NX * NZ - 1, xz2_sem)
+    exchange(plane_buf, (x * NZ + z) * 2 + core, row, plane_peers, plane_sem)
+    row = finish(plane_buf, 2 * NX * NZ - 1, plane_sem)
     exchange(y_buf, h * NLO + yl, row, y_peers, y_sem)
 
     for i, k in ((1, 1), (2, 3), (0, 2)):
@@ -483,13 +488,12 @@
             pltpu.VMEM((LAYERS, 2, ROWS // 2, 128), f32),
             pltpu.VMEM((NHI - 1, LAYERS, 2, piece, 128), f32),
             pltpu.VMEM(halved, f32),
-            pltpu.VMEM((NLO, 1, 128), f32),
-            pltpu.VMEM((NX * NZ, 1, 128), f32),
+            pltpu.VMEM((SPACE, 1, 128), f32),
             pltpu.VMEM((NHI * NLO, 1, 128), f32),
             pltpu.VMEM((2 * NX * NZ, 1, 128), f32),
         ]
-        + [dma((n,)) for n in (15, 8, 8, 2, 2, 2, 2, 4, 4, 3, 3, 3, 3, 4, 4)]
-        + [dma],
+        + [dma((n,)) for n in (15, 8, 8, 2, 2, 2, 4, 4, 3, 3, 3, 3, 4, 4)]
+        + [dma, pltpu.SemaphoreType.REGULAR((2,))],
         compiler_params=pltpu.CompilerParams(collective_id=0, has_side_effects=True, vmem_limit_bytes=24 << 20),
         name="step",
     )(*pinned)

time: 55.8 us -> 53.5 us (0.959)
  Pallas kernels: 55 us -> 52.6 us
    pallas_call x1, Pallas kernels: 53.6 us -> 51.1 us  [shards(): pl.pallas_call(kernel, out_shape=(jax.ShapeDtypeStruct(halved, f32), jax....]
where the time goes in v3:
time: 53.5 us; the launch traced here: 53.2 us
  Pallas kernels  52.6 us (98%)
  between operations  0.66 us (1%)
    pallas_call x1, Pallas kernels, shards(): pl.pallas_call(kernel, out_shape=(jax.ShapeDtypeStruct(halved, f32), jax....  51.1 us
    pallas_call x1, Pallas kernels, shards(): pl.pallas_call(update_kernel, out_shape=(jax.ShapeDtypeStruct(slab, f32),...  1.42 us

profile of v3, /device:TPU:1, one launch (start us, length us, event | category | flops | bytes accessed | tf_op | source)
XLA Modules:
  0.0 53.2 jit_solution(6506833656848337153)
XLA Ops:
  0.6 0.0 copy-start
  0.6 51.1 %step.1 = (f32[4,2,128,128]{3,2,1,0:T(8,128)S(1)}, f32[1,128]{1,0:T(1,128)S(1)}) custom-call(f32[4,128,256]{2,1,0:T(8,128)} %mean_ref.1, f32[1,4,128,256]{3,2,1,0:T(8,128)} %pert_hbm.1, f32[1,4,128,256]{3,2,1,0:T(8,128)} %conc_hbm.1, s32[1,4,128,256]{3,2,1,0:T(8,128)} %mask_hbm.1, s32[128,256]{1,0:T(8,128)} %ctrl_hbm.1, f32[1,8]{1,0:T(1,128)} %obs_hbm.1), custom_call_target="tpu_custom_call" | custom-call | tf_op jit(solution)/shard_map/step/pallas_call | solution.py:472
  51.8 0.0 copy-done
  51.8 1.4 %update.1 = (f32[4,128,256]{2,1,0:T(8,128)}, f32[1,1]{1,0:T(1,128)}) custom-call(f32[1,128]{1,0:T(1,128)S(1)} %get-tuple-element.6.row_ref, f32[4,128,256]{2,1,0:T(8,128)S(1)} %copy-done, f32[4,2,128,128]{3,2,1,0:T(8,128)S(1)} %get-tuple-element.7.tot_ref), custom_call_target="tpu_custom_call" | custom-call | tf_op jit(solution)/shard_map/update/pallas_call | solution.py:500
Async XLA Ops:
  0.6 51.2 %copy-start = (f32[4,128,256]{2,1,0:T(8,128)S(1)}, f32[4,128,256]{2,1,0:T(8,128)}, u32[]{:S(2)}) copy-start(f32[4,128,256]{2,1,0:T(8,128)} %mean_ref.1) | copy-start | bytes 1572868

commit v4 on v3

--- a/solution.py
+++ b/solution.py
@@ -60,9 +60,6 @@
     h_near = [dev(lax.rem(h + dh, NHI) * 2 + core, s) for dh in (1, NHI - 1)]
     beside = [dev(m, place(0, 1, 0)), sibling]
     near = [dev(m, right), dev(m, left)] + z_ring + x_ring + h_near + beside
-    barrier = pltpu.get_barrier_semaphore()
-    greet(barrier, near)
-
     inside = pl.ds(PAD, ROWS)
     edges = (0, LAYERS - 1)
     loads = {}
@@ -71,28 +68,51 @@
         loads[name] = pltpu.make_async_copy(src, dst, load_sem.at[index])
         loads[name].start()
 
+    barrier = pltpu.get_barrier_semaphore()
+    greet(barrier, near)
     for i, l in enumerate(edges):
         load(("m", l), i, mean_hbm.at[l], mean.at[l])
         load(("p", l), 2 + i, pert_hbm.at[0, l], pert.at[l])
     halves = (pl.ds(0, 128), pl.ds(128, 128))
-    for i, l in enumerate(edges):
-        for k, lanes in enumerate(halves):
-            load(("c", l, k), 4 + 2 * i + k, conc_hbm.at[0, l, :, lanes], C.at[l + 1, k, inside])
+    pl.semaphore_wait(barrier, len(near))
+
+    def halo(pairs, first):
+        copies = []
+        for i, (low, high, at_left, at_right) in enumerate(pairs):
+            for j, (src, dst, to) in enumerate(((high, at_right, right), (low, at_left, left))):
+                n = first + 2 * i + j
+                copies.append(
+                    pltpu.make_async_remote_copy(
+                        src_ref=src, dst_ref=dst, send_sem=halo_s.at[n], recv_sem=halo_r.at[n],
+                        device_id=dev(m, to), device_id_type=MESH,
+                    )
+                )
+                copies[-1].start()
+        return copies
+
+    def layers_of(ref):
+        return tuple(ref.at[e, :, inside] for e in (1, LAYERS, LAYERS + 1, 0))
+
+    halo_1 = halo(
+        [
+            (*(conc_hbm.at[0, l, :, lanes] for l in edges), C.at[LAYERS + 1, k, inside], C.at[0, k, inside])
+            for k, lanes in enumerate(halves)
+        ],
+        0,
+    )
+    greet(relay.at[0], x_ring + h_near)
+
     mid = pl.ds(1, LAYERS - 2)
     load("ctrl", 8, ctrl_hbm, ctrl)
     load("m", 9, mean_hbm.at[mid], mean.at[mid])
     load("p", 10, pert_hbm.at[0, mid], pert.at[mid])
+    for i, l in enumerate(edges):
+        for k, lanes in enumerate(halves):
+            load(("c", l, k), 4 + 2 * i + k, conc_hbm.at[0, l, :, lanes], C.at[l + 1, k, inside])
     for k, lanes in enumerate(halves):
         load(("c", k), 11 + k, conc_hbm.at[0, mid, :, lanes], C.at[pl.ds(2, LAYERS - 2), k, inside])
     load("mask", 13, mask_hbm.at[0], mask)
     load("obs", 14, obs_hbm, obs_ref)
-
-    zero_rows = jnp.zeros((2, PAD, 128), jnp.float32)
-    for ref in (K, C, U, D, Pf):
-        for e in range(LAYERS + 2):
-            ref[e, :, 0:PAD, :] = zero_rows
-            ref[e, :, PAD + ROWS : 2 * PAD + ROWS, :] = zero_rows
-    acc[...] = jnp.zeros_like(acc)
 
     def own_rows(b):
         return pl.ds(pl.multiple_of(b * BLOCK, BLOCK), BLOCK)
@@ -239,30 +259,14 @@
         loads[("m", l)].wait()
         loads[("p", l)].wait()
     each(OUTER, conductivity)
-    for l in edges:
-        for k in (0, 1):
-            loads[("c", l, k)].wait()
-    pl.semaphore_wait(barrier, len(near))
-    greet(relay.at[0], x_ring + h_near)
-
-    def halo(pairs, first):
-        copies = []
-        for i, (low, high, at_left, at_right) in enumerate(pairs):
-            for j, (src, dst, to) in enumerate(((high, at_right, right), (low, at_left, left))):
-                n = first + 2 * i + j
-                copies.append(
-                    pltpu.make_async_remote_copy(
-                        src_ref=src, dst_ref=dst, send_sem=halo_s.at[n], recv_sem=halo_r.at[n],
-                        device_id=dev(m, to), device_id_type=MESH,
-                    )
-                )
-                copies[-1].start()
-        return copies
-
-    def layers_of(ref):
-        return tuple(ref.at[e, :, inside] for e in (1, LAYERS, LAYERS + 1, 0))
-
-    halo_1 = halo((layers_of(K), layers_of(C)), 0)
+    halo_1 += halo((layers_of(K),), 4)
+
+    zero_rows = jnp.zeros((2, PAD, 128), jnp.float32)
+    for ref in (K, C, U, D, Pf):
+        for e in range(LAYERS + 2):
+            ref[e, :, 0:PAD, :] = zero_rows
+            ref[e, :, PAD + ROWS : 2 * PAD + ROWS, :] = zero_rows
+    acc[...] = jnp.zeros_like(acc)
     loads["m"].wait()
     loads["p"].wait()
     each(INNER, conductivity)
@@ -270,13 +274,18 @@
     greet(relay.at[1], beside)
     loads["ctrl"].wait()
     each(OWN, selected)
+    for l in edges:
+        for k in (0, 1):
+            loads[("c", l, k)].wait()
     for k in (0, 1):
         loads[("c", k)].wait()
     loads["mask"].wait()
     loads["obs"].wait()
     each(OUTER, transport_outer)
-    halo_2 = halo(((Dp.at[0], Dp.at[1], *layers_of(D)[2:]),), 4)
     each(INNER, transport_inner)
+    for copy in halo_1:
+        copy.wait_send()
+    halo_2 = halo(((Dp.at[0], Dp.at[1], *layers_of(D)[2:]),), 6)
     cross_in = [crossing_terms(e) for e in range(2, LAYERS)]
 
     def clear(refs):
@@ -328,7 +337,7 @@
 
     pl.semaphore_wait(relay.at[1], len(beside))
     exchange(space_buf, s, to_row(column), space_peers, space_sem)
-    halo_2 += halo((layers_of(Pf),), 6)
+    halo_2 += halo((layers_of(Pf),), 8)
 
     each(INNER, gradient_inner)
     each(OUTER, gradient_outer)
@@ -439,7 +448,7 @@
         copy.wait_recv()
     out = pltpu.make_async_copy(tot, tot_ref, out_sem)
     out.start()
-    for copy in halo_1 + halo_2 + cores + scatter + gather + handed:
+    for copy in halo_2 + cores + scatter + gather + handed:
         copy.wait_send()
     row = finish(y_buf, NHI * NLO - 1, y_sem)
     row_ref[...] = row
@@ -447,14 +456,15 @@
 
 
 def update_kernel(row_ref, mean_ref, tot_ref, out_ref, misfit_ref):
-    squares = jnp.full((8, 128), row_ref[0, 0])
+    lane = lax.broadcasted_iota(jnp.int32, (1, 128), 1)
+    squares = jnp.broadcast_to(jnp.sum(jnp.where(lane == 0, row_ref[...], 0.0), axis=1, keepdims=True), (8, 128))
     scale = descent_rate * lax.rsqrt(squares * (1.0 / (SPACE * LAYERS * ROWS * LANES)) + epsilon)
     for l in range(LAYERS):
         for r in range(0, ROWS, 8):
             for k in (0, 1):
                 lanes = slice(128 * k, 128 * k + 128)
                 out_ref[l, r : r + 8, lanes] = mean_ref[l, r : r + 8, lanes] - scale * tot_ref[l, k, r : r + 8, :]
-    misfit_ref[0, 0] = row_ref[0, 1] * (0.5 / (MEMBERS * NOBS * SPACE))
+    misfit_ref[0, 0] = jnp.sum(jnp.where(lane == 1, row_ref[...], 0.0)) * (0.5 / (MEMBERS * NOBS * SPACE))
 
 
 def shards(mean_logk, perturbation, start_conc, source_mask, control_x, observed):
@@ -492,7 +502,7 @@
             pltpu.VMEM((NHI * NLO, 1, 128), f32),
             pltpu.VMEM((2 * NX * NZ, 1, 128), f32),
         ]
-        + [dma((n,)) for n in (15, 8, 8, 2, 2, 2, 4, 4, 3, 3, 3, 3, 4, 4)]
+        + [dma((n,)) for n in (15, 10, 10, 2, 2, 2, 4, 4, 3, 3, 3, 3, 4, 4)]
         + [dma, pltpu.SemaphoreType.REGULAR((2,))],
         compiler_params=pltpu.CompilerParams(collective_id=0, has_side_effects=True, vmem_limit_bytes=24 << 20),
         name="step",
@@ -500,7 +510,7 @@
     updated, misfit = pl.pallas_call(
         update_kernel,
         out_shape=(jax.ShapeDtypeStruct(slab, f32), jax.ShapeDtypeStruct((1, 1), f32)),
-        in_specs=[smem, vmem, vmem],
+        in_specs=[vmem, vmem, vmem],
         out_specs=(vmem, smem),
         compiler_params=pltpu.CompilerParams(vmem_limit_bytes=8 << 20),
         name="update",

time: 53.5 us -> 52.7 us (0.985)
  Pallas kernels: 52.6 us -> 51.8 us
where the time goes in v4:
time: 52.7 us; the launch traced here: 52.4 us
  Pallas kernels  51.8 us (98%)
  between operations  0.66 us (1%)
    pallas_call x1, Pallas kernels, shards(): pl.pallas_call(kernel, out_shape=(jax.ShapeDtypeStruct(halved, f32), jax....  50.8 us

profile of v4, /device:TPU:1, one launch (start us, length us, event | category | flops | bytes accessed | tf_op | source)
XLA Modules:
  0.0 52.4 jit_solution(7188501048609900205)
XLA Ops:
  0.6 0.0 copy-start
  0.6 50.8 %step.1 = (f32[4,2,128,128]{3,2,1,0:T(8,128)S(1)}, f32[1,128]{1,0:T(1,128)S(1)}) custom-call(f32[4,128,256]{2,1,0:T(8,128)} %mean_ref.1, f32[1,4,128,256]{3,2,1,0:T(8,128)} %pert_hbm.1, f32[1,4,128,256]{3,2,1,0:T(8,128)} %conc_hbm.1, s32[1,4,128,256]{3,2,1,0:T(8,128)} %mask_hbm.1, s32[128,256]{1,0:T(8,128)} %ctrl_hbm.1, f32[1,8]{1,0:T(1,128)} %obs_hbm.1), custom_call_target="tpu_custom_call" | custom-call | tf_op jit(solution)/shard_map/step/pallas_call | solution.py:482
  51.5 0.0 copy-done
  51.5 1.0 %update.1 = (f32[4,128,256]{2,1,0:T(8,128)}, f32[1,1]{1,0:T(1,128)}) custom-call(f32[1,128]{1,0:T(1,128)S(1)} %get-tuple-element.6.row_ref, f32[4,128,256]{2,1,0:T(8,128)S(1)} %copy-done, f32[4,2,128,128]{3,2,1,0:T(8,128)S(1)} %get-tuple-element.7.tot_ref), custom_call_target="tpu_custom_call" | custom-call | tf_op jit(solution)/shard_map/update/pallas_call | solution.py:510
Async XLA Ops:
  0.6 50.8 %copy-start = (f32[4,128,256]{2,1,0:T(8,128)S(1)}, f32[4,128,256]{2,1,0:T(8,128)}, u32[]{:S(2)}) copy-start(f32[4,128,256]{2,1,0:T(8,128)} %mean_ref.1) | copy-start | bytes 1572868

commit v5 on v4

--- a/solution.py
+++ b/solution.py
@@ -393,47 +393,56 @@
             )
         )
         cores[-1].start()
-    scatter = []
+    parts_of = (pl.ds(0, LAYERS // 2), pl.ds(LAYERS // 2, LAYERS // 2))
+    scatter = ([], [])
+
+    def send_part(q, i, chip):
+        copy = pltpu.make_async_remote_copy(
+            src_ref=hsum.at[parts_of[q], :, piece_of(chip), :], dst_ref=rs.at[i, parts_of[q]],
+            send_sem=rs_s.at[3 * q + i], recv_sem=rs_r.at[3 * q + i],
+            device_id=dev(chip * 2 + core, s), device_id_type=MESH,
+        )
+        copy.start()
+        scatter[q].append(copy)
+
     for i, k in enumerate(order):
         chip = lax.rem(h + k, NHI)
         cores[i].wait_recv()
         hsum[:, :, piece_of(chip), :] = G[:, :, rows_of(core, chip), :] + sib[:, :, piece_of(chip), :]
         if k:
-            scatter.append(
-                pltpu.make_async_remote_copy(
-                    src_ref=hsum.at[:, :, piece_of(chip), :], dst_ref=rs.at[i],
-                    send_sem=rs_s.at[i], recv_sem=rs_r.at[i],
-                    device_id=dev(chip * 2 + core, s), device_id_type=MESH,
-                )
-            )
-            scatter[-1].start()
-    for copy in scatter:
-        copy.wait_recv()
-    total = hsum[:, :, piece_of(h), :] + rs[0] + rs[1] + rs[2]
-    tot[:, :, rows_of(core, h), :] = total
-
-    def hand_on(chip, i):
-        part = tot.at[:, :, rows_of(core, chip), :]
+            send_part(0, i, chip)
+    for i, k in enumerate(order):
+        if k:
+            send_part(1, i, lax.rem(h + k, NHI))
+
+    def hand_on(q, chip, i):
+        part = tot.at[parts_of[q], :, rows_of(core, chip), :]
         copy = pltpu.make_async_remote_copy(
-            src_ref=part, dst_ref=part, send_sem=sg_s.at[i], recv_sem=sg_r.at[i],
+            src_ref=part, dst_ref=part, send_sem=sg_s.at[4 * q + i], recv_sem=sg_r.at[4 * q + i],
             device_id=sibling, device_id_type=MESH,
         )
         copy.start()
         return copy
 
-    gather = []
-    mine = tot.at[:, :, rows_of(core, h), :]
-    for i, k in enumerate((2, 1, 3)):
-        gather.append(
-            pltpu.make_async_remote_copy(
-                src_ref=mine, dst_ref=mine, send_sem=ag_s.at[i], recv_sem=ag_r.at[i],
+    gather, handed = ([], []), []
+    squares = jnp.zeros((piece, 128), jnp.float32)
+    for q in (0, 1):
+        for copy in scatter[q]:
+            copy.wait_recv()
+        total = hsum[parts_of[q], :, piece_of(h), :] + rs[0, parts_of[q]] + rs[1, parts_of[q]] + rs[2, parts_of[q]]
+        tot[parts_of[q], :, rows_of(core, h), :] = total
+        mine = tot.at[parts_of[q], :, rows_of(core, h), :]
+        for i, k in enumerate((2, 1, 3)):
+            copy = pltpu.make_async_remote_copy(
+                src_ref=mine, dst_ref=mine, send_sem=ag_s.at[3 * q + i], recv_sem=ag_r.at[3 * q + i],
                 device_id=dev(lax.rem(h + k, NHI) * 2 + core, s), device_id_type=MESH,
             )
-        )
-        gather[-1].start()
-    handed = [hand_on(h, 0)]
-
-    squares = jnp.sum(jnp.sum(total * total, axis=(0, 1)), axis=0, keepdims=True)
+            copy.start()
+            gather[q].append(copy)
+        handed.append(hand_on(q, h, 0))
+        squares = squares + jnp.sum(total * total, axis=(0, 1))
+
+    squares = jnp.sum(squares, axis=0, keepdims=True)
     squares = jnp.sum(squares, axis=1, keepdims=True)
     lane_row = lax.broadcasted_iota(jnp.int32, (1, 128), 1)
     row = jnp.where(lane_row == 0, squares, jnp.where(lane_row == 1, misfit, 0.0))
@@ -441,14 +450,15 @@
     row = finish(plane_buf, 2 * NX * NZ - 1, plane_sem)
     exchange(y_buf, h * NLO + yl, row, y_peers, y_sem)
 
-    for i, k in ((1, 1), (2, 3), (0, 2)):
-        gather[i].wait_recv()
-        handed.append(hand_on(lax.rem(h + NHI - k, NHI), i + 1))
+    for q in (0, 1):
+        for i, k in ((1, 1), (2, 3), (0, 2)):
+            gather[q][i].wait_recv()
+            handed.append(hand_on(q, lax.rem(h + NHI - k, NHI), i + 1))
     for copy in handed:
         copy.wait_recv()
     out = pltpu.make_async_copy(tot, tot_ref, out_sem)
     out.start()
-    for copy in halo_2 + cores + scatter + gather + handed:
+    for copy in halo_2 + cores + scatter[0] + scatter[1] + gather[0] + gather[1] + handed:
         copy.wait_send()
     row = finish(y_buf, NHI * NLO - 1, y_sem)
     row_ref[...] = row
@@ -502,7 +512,7 @@
             pltpu.VMEM((NHI * NLO, 1, 128), f32),
             pltpu.VMEM((2 * NX * NZ, 1, 128), f32),
         ]
-        + [dma((n,)) for n in (15, 10, 10, 2, 2, 2, 4, 4, 3, 3, 3, 3, 4, 4)]
+        + [dma((n,)) for n in (15, 10, 10, 2, 2, 2, 4, 4, 6, 6, 6, 6, 8, 8)]
         + [dma, pltpu.SemaphoreType.REGULAR((2,))],
         compiler_params=pltpu.CompilerParams(collective_id=0, has_side_effects=True, vmem_limit_bytes=24 << 20),
         name="step",

time: 52.7 us -> 54.5 us (1.034)
  Pallas kernels: 51.8 us -> 53.7 us
    pallas_call x1, Pallas kernels: 50.8 us -> 52.7 us  [shards(): pl.pallas_call(kernel, out_shape=(jax.ShapeDtypeStruct(halved, f32), jax....]
where the time goes in v5:
time: 54.5 us; the launch traced here: 54.4 us
  Pallas kernels  53.7 us (99%)
  between operations  0.66 us (1%)
    pallas_call x1, Pallas kernels, shards(): pl.pallas_call(kernel, out_shape=(jax.ShapeDtypeStruct(halved, f32), jax....  52.7 us

profile of v5, /device:TPU:1, one launch (start us, length us, event | category | flops | bytes accessed | tf_op | source)
XLA Modules:
  0.0 54.4 jit_solution(6773371913297865592)
XLA Ops:
  0.6 0.0 copy-start
  0.6 52.7 %step.1 = (f32[4,2,128,128]{3,2,1,0:T(8,128)S(1)}, f32[1,128]{1,0:T(1,128)S(1)}) custom-call(f32[4,128,256]{2,1,0:T(8,128)} %mean_ref.1, f32[1,4,128,256]{3,2,1,0:T(8,128)} %pert_hbm.1, f32[1,4,128,256]{3,2,1,0:T(8,128)} %conc_hbm.1, s32[1,4,128,256]{3,2,1,0:T(8,128)} %mask_hbm.1, s32[128,256]{1,0:T(8,128)} %ctrl_hbm.1, f32[1,8]{1,0:T(1,128)} %obs_hbm.1), custom_call_target="tpu_custom_call" | custom-call | tf_op jit(solution)/shard_map/step/pallas_call | solution.py:492
  53.4 0.0 copy-done
  53.4 1.0 %update.1 = (f32[4,128,256]{2,1,0:T(8,128)}, f32[1,1]{1,0:T(1,128)}) custom-call(f32[1,128]{1,0:T(1,128)S(1)} %get-tuple-element.6.row_ref, f32[4,128,256]{2,1,0:T(8,128)S(1)} %copy-done, f32[4,2,128,128]{3,2,1,0:T(8,128)S(1)} %get-tuple-element.7.tot_ref), custom_call_target="tpu_custom_call" | custom-call | tf_op jit(solution)/shard_map/update/pallas_call | solution.py:520
Async XLA Ops:
  0.6 52.8 %copy-start = (f32[4,128,256]{2,1,0:T(8,128)S(1)}, f32[4,128,256]{2,1,0:T(8,128)}, u32[]{:S(2)}) copy-start(f32[4,128,256]{2,1,0:T(8,128)} %mean_ref.1) | copy-start | bytes 1572868

commit v6 on v4

--- a/solution.py
+++ b/solution.py
@@ -255,11 +255,18 @@
             bnd[e - 1, 2 * i] = -HALF * k * bracket
             bnd[e - 1, 2 * i + 1] = -HALF * strided(K, e, further) * (q * (c - c_further))
 
-    for l in edges:
-        loads[("m", l)].wait()
-        loads[("p", l)].wait()
-    each(OUTER, conductivity)
-    halo_1 += halo((layers_of(K),), 4)
+    low, high, at_left, at_right = layers_of(K)
+    for n, e, src, dst, to in ((4, LAYERS, high, at_right, right), (5, 1, low, at_left, left)):
+        loads[("m", e - 1)].wait()
+        loads[("p", e - 1)].wait()
+        each((e, 1, 1), conductivity)
+        halo_1.append(
+            pltpu.make_async_remote_copy(
+                src_ref=src, dst_ref=dst, send_sem=halo_s.at[n], recv_sem=halo_r.at[n],
+                device_id=dev(m, to), device_id_type=MESH,
+            )
+        )
+        halo_1[-1].start()
 
     zero_rows = jnp.zeros((2, PAD, 128), jnp.float32)
     for ref in (K, C, U, D, Pf):

time: 52.7 us -> 52.7 us (level)
  no operation moved by 1% of the time
where the time goes in v6:
time: 52.7 us; the launch traced here: 52.4 us
  Pallas kernels  51.8 us (98%)
  between operations  0.66 us (1%)
    pallas_call x1, Pallas kernels, shards(): pl.pallas_call(kernel, out_shape=(jax.ShapeDtypeStruct(halved, f32), jax....  50.8 us

profile of v6, /device:TPU:1, one launch (start us, length us, event | category | flops | bytes accessed | tf_op | source)
XLA Modules:
  0.0 52.4 jit_solution(5005461590646164343)
XLA Ops:
  0.6 0.0 copy-start
  0.6 50.8 %step.1 = (f32[4,2,128,128]{3,2,1,0:T(8,128)S(1)}, f32[1,128]{1,0:T(1,128)S(1)}) custom-call(f32[4,128,256]{2,1,0:T(8,128)} %mean_ref.1, f32[1,4,128,256]{3,2,1,0:T(8,128)} %pert_hbm.1, f32[1,4,128,256]{3,2,1,0:T(8,128)} %conc_hbm.1, s32[1,4,128,256]{3,2,1,0:T(8,128)} %mask_hbm.1, s32[128,256]{1,0:T(8,128)} %ctrl_hbm.1, f32[1,8]{1,0:T(1,128)} %obs_hbm.1), custom_call_target="tpu_custom_call" | custom-call | tf_op jit(solution)/shard_map/step/pallas_call | solution.py:489
  51.5 0.0 copy-done
  51.5 1.0 %update.1 = (f32[4,128,256]{2,1,0:T(8,128)}, f32[1,1]{1,0:T(1,128)}) custom-call(f32[1,128]{1,0:T(1,128)S(1)} %get-tuple-element.6.row_ref, f32[4,128,256]{2,1,0:T(8,128)S(1)} %copy-done, f32[4,2,128,128]{3,2,1,0:T(8,128)S(1)} %get-tuple-element.7.tot_ref), custom_call_target="tpu_custom_call" | custom-call | tf_op jit(solution)/shard_map/update/pallas_call | solution.py:517
Async XLA Ops:
  0.6 50.8 %copy-start = (f32[4,128,256]{2,1,0:T(8,128)S(1)}, f32[4,128,256]{2,1,0:T(8,128)}, u32[]{:S(2)}) copy-start(f32[4,128,256]{2,1,0:T(8,128)} %mean_ref.1) | copy-start | bytes 1572868
